TPU v7x, 128 devices: a whole 4x4x4 slice. The times are simulated.
128 devices in a mesh: section: 8 (over x_hi, y), feat: 16 (over x_lo, z, core).
Axes of the slice: x: 4 (x_hi: 2, x_lo: 2; x = x_hi * 2 + x_lo), y: 4, z: 4, core: 2. Of those that a mesh axis runs over, the one named last changes fastest.
Arguments:
- resid_in: bfloat16 [1024, 8192], P('feat', 'section'), may hold values from -6 to 6
- active: int32 [1024, 24], replicated, may hold values from 0 to 255, all different within a row; in each aligned block of 64 rows (0 to 63, 64 to 127, ...) at most 24 rows name the same one
- enc_weight: bfloat16 [8192, 32768], P('section', 'feat'), may hold values from -0.0625 to 0.0625
- enc_bias: float32 [32768], P('feat'), may hold values from -3 to 3
- dec_weight: bfloat16 [8, 32768, 4096], P('section', 'feat'), may hold values from -0.109375 to 0.109375
- target_resid: bfloat16 [8, 1024, 4096], P('section', 'feat'), may hold values from -6 to 6
- slot_block: int32 [256], replicated, may hold values from 0 to 255, each once
- source: int32 [1024], P('feat'), may hold values from 0 to 7
Outputs:
- recon_error: bfloat16 [8, 1024, 4096], P('section', 'feat')
Inputs may be any that keep to these rules, and one draw needn't show every extreme that they name: `active`: each token names 24 different blocks. Among the 64 tokens of one feat index (aligned blocks of 64 rows) no block is named by more than 24 tokens, and some block by exactly 24. `slot_block`: every block number appears once.
All inputs are finite; a program needn't handle non-finite values.
Results may differ from a plain program's by a relative error of at most 0.019.
Values may be sent and summed in bfloat16 or wider, within the bound.
No kernel may reach another device: no remote copies, remote signals or barrier semaphores. Data moves between devices by JAX's collectives and lax.ppermute only.
A program may use at most 128 MiB of HBM per device.

v0:
```python
import functools

import jax
import jax.numpy as jnp
from jax import lax
from jax.experimental import pallas as pl
from jax.experimental.pallas import tpu as pltpu
from jax.sharding import PartitionSpec as P

BLK = 128
GRP = 64
CAP = 384
TOK = 1024
NPOS = 256
OWN = 16
FULL = OWN * CAP
SMALL = FULL // 2
WIN = 128
HALF = 512
XL, Z, C = 2, 4, 2
BF = jnp.bfloat16
F32 = jnp.float32
I32 = jnp.int32
VM = pl.BlockSpec(memory_space=pltpu.VMEM)
SM = pl.BlockSpec(memory_space=pltpu.SMEM)
ANY = pl.BlockSpec(memory_space=pl.ANY)


def feat_perm(move):
    pairs = []
    for xl in range(XL):
        for z in range(Z):
            for c in range(C):
                a, b, d = move(xl, z, c)
                pairs.append(((xl * Z + z) * C + c, (a * Z + b) * C + d))
    return pairs


UP = feat_perm(lambda xl, z, c: (xl, (z + 1) % Z, c))
DOWN = feat_perm(lambda xl, z, c: (xl, (z + Z - 1) % Z, c))
SWAP_X = feat_perm(lambda xl, z, c: (1 - xl, z, c))
SWAP_C = feat_perm(lambda xl, z, c: (xl, z, 1 - c))
SAME_C = [[(xl * Z + z) * C + c for xl in range(XL) for z in range(Z)] for c in range(C)]


def move(x, pairs):
    return lax.ppermute(x, "feat", pairs)


def iota(shape, dim):
    return lax.broadcasted_iota(I32, shape, dim)


def index_kernel(where_ref, active_ref, slot_ref, rows_ref, cols_ref, meta_ref, most_ref, hits, rowt):
    f = where_ref[0]
    xl, z, c = f // (Z * C), (f // C) % Z, f % C
    for p in range(0, NPOS, 32):
        slots = jnp.broadcast_to(slot_ref[p : p + 32, :], (32, 128))
        for t in range(0, TOK, 128):
            named = active_ref[:, t : t + 128]
            hit = named[0:1, :] == slots
            for k in range(1, active_ref.shape[0]):
                hit = jnp.logical_or(hit, named[k : k + 1, :] == slots)
            hits[p : p + 32, t : t + 128] = jnp.where(hit, 1.0, 0.0).astype(BF)
    ones = jnp.ones((TOK, 128), BF)
    every = jnp.dot(hits[...], ones, preferred_element_type=F32)
    group = jnp.where(iota((OWN, NPOS), 1) // OWN == iota((OWN, NPOS), 0), 1.0, 0.0).astype(BF)
    units = jnp.floor((every + 15.0) * (1.0 / 16.0)).astype(BF)
    totals = jnp.dot(group, units, preferred_element_type=F32) * 16.0
    most_ref[0, 0] = jnp.max(totals).astype(I32)
    other = f + 1 - 2 * c
    mine = jnp.concatenate(
        [hits[pl.ds(pl.multiple_of(o * OWN, OWN), OWN), :] for o in (f, other)], axis=0
    )
    tiles = TOK // 128
    stack = jnp.concatenate([mine[:, t * 128 : (t + 1) * 128] for t in range(tiles)], axis=0)
    i, j = iota((128, 128), 0), iota((128, 128), 1)
    inside = jnp.dot(stack, jnp.where(i < j, 1.0, 0.0).astype(BF), preferred_element_type=F32)
    sums = jnp.dot(stack, jnp.ones((128, 128), BF), preferred_element_type=F32)
    n = 2 * OWN
    running = [jnp.zeros((n, 128), F32)]
    for t in range(tiles):
        running.append(running[-1] + sums[t * n : (t + 1) * n])
    counts = running[-1]
    own_units = jnp.floor((counts + 15.0) * (1.0 / 16.0)).astype(BF)
    ci, cj = iota((n, n), 0), iota((n, n), 1)
    chain = jnp.where((cj < ci) & (ci // OWN == cj // OWN), 1.0, 0.0).astype(BF)
    starts = jnp.dot(chain, own_units, preferred_element_type=F32) * 16.0
    placed = [
        jnp.where(
            stack[t * n : (t + 1) * n].astype(F32) > 0.5,
            inside[t * n : (t + 1) * n] + running[t] + starts,
            -1.0,
        )
        for t in range(tiles)
    ]
    low = iota((n, 128), 1) < GRP
    for t in range(tiles // 2):
        even, odd = placed[2 * t], placed[2 * t + 1]
        core0 = jnp.where(low, even, pltpu.roll(odd, GRP, 1))
        core1 = jnp.where(low, pltpu.roll(even, GRP, 1), odd)
        near, far = jnp.where(c == 0, core0, core1), jnp.where(c == 0, core1, core0)
        rows_ref[:, t * 128 : (t + 1) * 128] = near.astype(I32)
        rows_ref[:, HALF + t * 128 : HALF + (t + 1) * 128] = far.astype(I32)
    blank = jnp.full((128 - n, 128), -1.0, F32)
    for t in range(tiles):
        tall = jnp.transpose(jnp.concatenate([placed[t], blank], axis=0))
        rowt[t * 128 : (t + 1) * 128, :] = tall.astype(I32)
    for xr in range(XL):
        for zr in range(Z):
            g = ((xl + xr) % XL * Z + (z + zr) % Z) * C + c
            to = (xr * Z + zr) * GRP
            cols_ref[to : to + GRP, :] = rowt[pl.ds(pl.multiple_of(g * GRP, GRP), GRP), :]
    flat = jnp.transpose(jnp.concatenate([starts, counts, jnp.zeros((64, 128), F32)], axis=0))
    meta_ref[...] = flat[0:8, :].astype(I32)


def index_call(where, active, slots):
    return pl.pallas_call(
        index_kernel,
        in_specs=[SM, VM, VM],
        out_specs=[VM, VM, VM, SM],
        out_shape=[
            jax.ShapeDtypeStruct((2 * OWN, TOK), I32),
            jax.ShapeDtypeStruct((HALF, 128), I32),
            jax.ShapeDtypeStruct((8, 128), I32),
            jax.ShapeDtypeStruct((1, 1), I32),
        ],
        scratch_shapes=[pltpu.VMEM((NPOS, TOK), BF), pltpu.VMEM((TOK, 128), I32)],
        compiler_params=pltpu.CompilerParams(vmem_limit_bytes=32 << 20),
        cost_estimate=pl.CostEstimate(flops=4 << 30, bytes_accessed=1 << 20, transcendentals=0),
    )(where, active, slots)


def encode_kernel(meta_ref, near_ref, far_ref, rows_ref, enc_ref, out_ref, held):
    first = pl.program_id(0) * 2

    def pack(b, w):
        at = pl.multiple_of(meta_ref[0, first + b] + w * WIN, 16)
        place = rows_ref[pl.ds(first + b, 1), :]
        one = jnp.where(iota((WIN, TOK), 0) == place - at, 1.0, 0.0).astype(BF)
        part = held[:, b * BLK : (b + 1) * BLK]
        out_ref[pl.ds(at, WIN), :] = jnp.dot(one, part, preferred_element_type=F32).astype(BF)

    enc = enc_ref[...]
    held[:HALF, :] = jnp.dot(near_ref[...], enc, preferred_element_type=F32).astype(BF)
    held[HALF:, :] = jnp.dot(far_ref[...], enc, preferred_element_type=F32).astype(BF)
    for b in range(2):
        pack(b, 0)
        for w in range(1, CAP // WIN):

            @pl.when(meta_ref[0, 2 * OWN + first + b] > w * WIN)
            def _(b=b, w=w):
                pack(b, w)


def encode_call(meta, near, far, rows, enc):
    return pl.pallas_call(
        encode_kernel,
        grid=(OWN // 2,),
        in_specs=[
            SM,
            pl.BlockSpec(near.shape, lambda i: (0, 0)),
            pl.BlockSpec(far.shape, lambda i: (0, 0)),
            pl.BlockSpec((2 * OWN, TOK), lambda i: (0, 0)),
            pl.BlockSpec((enc.shape[0], 2 * BLK), lambda i: (0, i)),
        ],
        out_specs=pl.BlockSpec((FULL, BLK), lambda i: (0, 0)),
        out_shape=jax.ShapeDtypeStruct((FULL, BLK), BF),
        scratch_shapes=[pltpu.VMEM((TOK, 2 * BLK), BF)],
        compiler_params=pltpu.CompilerParams(
            vmem_limit_bytes=32 << 20, dimension_semantics=("arbitrary",)
        ),
        cost_estimate=pl.CostEstimate(flops=6 << 30, bytes_accessed=8 << 20, transcendentals=0),
    )(meta, near, far, rows, enc)


def reduce_kernel(where_ref, meta_ref, parts_ref, bias_ref, out_ref):
    share = out_ref.shape[0]
    total = parts_ref[0].astype(F32)
    for s in range(1, parts_ref.shape[0]):
        total = total + parts_ref[s].astype(F32)
    row = iota((share, BLK), 0) + where_ref[1] * share
    bias = jnp.zeros((share, BLK), F32)
    for b in range(OWN):
        bias = jnp.where(row >= meta_ref[0, b], bias_ref[b : b + 1, :], bias)
    last = meta_ref[0, OWN - 1] + meta_ref[0, 3 * OWN - 1]
    out_ref[...] = jnp.where(row < last, jnp.maximum(total + bias, 0.0), 0.0).astype(BF)


def reduce_call(where, meta, parts, bias):
    return pl.pallas_call(
        reduce_kernel,
        in_specs=[SM, SM, VM, VM],
        out_specs=VM,
        out_shape=jax.ShapeDtypeStruct(parts.shape[1:], BF),
        compiler_params=pltpu.CompilerParams(vmem_limit_bytes=32 << 20),
        cost_estimate=pl.CostEstimate(flops=16 << 20, bytes_accessed=4 << 20, transcendentals=0),
    )(where, meta, parts, bias)


def spread_kernel(first, meta_ref, cols_ref, act_ref, out_ref):
    rows = act_ref.shape[0]

    def window(begin, place, width):
        at = pl.multiple_of(jnp.minimum(begin, rows - width), 16)
        one = jnp.where(iota((HALF, width), 1) == place - at, 1.0, 0.0).astype(BF)
        part = act_ref[pl.ds(at, width), :]
        return jnp.dot(one, part, preferred_element_type=F32).astype(BF)

    cols = cols_ref[...]
    for b in range(OWN):
        place = cols[:, first + b : first + b + 1]
        out_ref[:, b * BLK : (b + 1) * BLK] = window(meta_ref[0, first + b], place, WIN)
    for b in range(OWN):
        start, count = meta_ref[0, first + b], meta_ref[0, 2 * OWN + first + b]

        @pl.when(count > WIN)
        def _(b=b, start=start):
            begin = start + WIN
            place = cols_ref[:, first + b : first + b + 1]
            place = jnp.where(place >= begin, place, -rows)
            out_ref[:, b * BLK : (b + 1) * BLK] += window(begin, place, CAP - WIN)


def spread_call(first, meta, cols, act):
    return pl.pallas_call(
        functools.partial(spread_kernel, first),
        in_specs=[SM, VM, VM],
        out_specs=VM,
        out_shape=jax.ShapeDtypeStruct((HALF, OWN * BLK), BF),
        compiler_params=pltpu.CompilerParams(vmem_limit_bytes=32 << 20),
        cost_estimate=pl.CostEstimate(flops=1 << 30, bytes_accessed=4 << 20, transcendentals=0),
    )(meta, cols, act)


def decode_kernel(kind, half, a1_ref, a2_ref, w1_ref, w2_ref, after_ref, *outs):
    y = jnp.dot(a1_ref[...], w1_ref[...], preferred_element_type=F32)
    y = y + jnp.dot(a2_ref[...], w2_ref[...], preferred_element_type=F32)
    y = y.astype(BF)
    if kind == "x":
        outs[0][...] = y[: HALF // 2]
        outs[1][...] = y[HALF // 2 :]
        return
    z2 = []
    for zr, out in ((0, outs[0]), (1, outs[1]), (3, outs[2])):
        out[0:GRP, :] = y[zr * GRP : (zr + 1) * GRP]
        out[GRP : 2 * GRP, :] = y[HALF // 2 + zr * GRP : HALF // 2 + (zr + 1) * GRP]
    step = pl.program_id(0)
    for out, here in ((outs[3], step < half), (outs[4], step >= half)):

        @pl.when(here)
        def _(out=out):
            out[0:GRP, :] = y[2 * GRP : 3 * GRP]
            out[GRP : 2 * GRP, :] = y[HALF // 2 + 2 * GRP : HALF // 2 + 3 * GRP]


def decode_call(kind, a1, a2, w1, w2, first, width, after, tile=512):
    steps, base = width // tile, first // tile
    half = steps // 2
    depth = w1.shape[0]
    weights = pl.BlockSpec((depth, tile), lambda i: (0, base + i))
    acts = pl.BlockSpec((HALF, depth), lambda i: (0, 0))
    if kind == "x":
        shapes = [(HALF // 2, width)] * 2
        specs = [pl.BlockSpec((HALF // 2, tile), lambda i: (0, i))] * 2
    else:
        shapes = [(2 * GRP, width)] * 3 + [(2 * GRP, half * tile), (2 * GRP, width - half * tile)]
        specs = [pl.BlockSpec((2 * GRP, tile), lambda i: (0, i))] * 3 + [
            pl.BlockSpec((2 * GRP, tile), lambda i: (0, jnp.minimum(i, half - 1))),
            pl.BlockSpec((2 * GRP, tile), lambda i: (0, jnp.maximum(i - half, 0))),
        ]
    return pl.pallas_call(
        functools.partial(decode_kernel, kind, half),
        grid=(steps,),
        in_specs=[acts, acts, weights, weights, ANY],
        out_specs=specs,
        out_shape=[jax.ShapeDtypeStruct(s, BF) for s in shapes],
        compiler_params=pltpu.CompilerParams(
            vmem_limit_bytes=40 << 20, dimension_semantics=("arbitrary",)
        ),
        cost_estimate=pl.CostEstimate(
            flops=4 * HALF * depth * width,
            bytes_accessed=4 * depth * width + HALF * width * 2 + 4 * HALF * depth,
            transcendentals=0,
        ),
    )(a1, a2, w1, w2, after)


def add(*terms):
    total = terms[0].astype(F32)
    for term in terms[1:]:
        total = total + term.astype(F32)
    return total


def ring_sum(z0, z1, z3, left, right):
    h = left.shape[1]
    got_left, got_right = move(left, UP), move(right, DOWN)
    up = jnp.concatenate([add(z1[:, :h], got_left).astype(BF), z1[:, h:]], axis=1)
    down = jnp.concatenate([z3[:, :h], add(z3[:, h:], got_right).astype(BF)], axis=1)
    return add(z0, move(up, UP), move(down, DOWN))


PLAN = (("x", 2048), ("z", 2048))


def body(resid_in, active, enc_weight, enc_bias, dec_weight, target_resid, slot_block, source):
    feat_index = lax.axis_index("feat")
    section_index = lax.axis_index("section")
    sections = lax.axis_size("section")
    where = jnp.stack([feat_index, section_index]).astype(I32)
    decoder = dec_weight[0]
    other_decoder = move(decoder, SWAP_C)
    rows, cols, meta, most = index_call(where, active.T, slot_block.reshape(NPOS, 1))
    copies = jnp.broadcast_to(resid_in[None], (XL * Z,) + resid_in.shape)
    near = lax.all_to_all(copies, "feat", 0, 0, axis_index_groups=SAME_C)
    near = near.reshape(HALF, resid_in.shape[1])
    packed = encode_call(meta, near, move(near, SWAP_C), rows, enc_weight)
    bias = enc_bias.reshape(OWN, BLK)

    def exchange(room, packed):
        share = room // sections
        parts = packed[:room].reshape(sections, share, BLK)
        parts = lax.all_to_all(parts, "section", 0, 0)
        mine = reduce_call(where, meta, parts, bias)
        wide = jnp.broadcast_to(mine[None], (sections, share, BLK))
        act = lax.all_to_all(wide, "section", 0, 0).reshape(room, BLK)
        return jnp.pad(act, ((0, FULL - room), (0, 0)))

    act = lax.cond(
        most[0, 0] <= SMALL,
        functools.partial(exchange, SMALL),
        functools.partial(exchange, FULL),
        packed,
    )
    theirs = move(act, SWAP_C)
    own = spread_call(0, meta, cols, act)
    theirs = spread_call(OWN, meta, cols, theirs)

    pieces, first, after = [], 0, meta
    for kind, width in PLAN:
        outs = decode_call(kind, own, theirs, decoder, other_decoder, first, width, after)
        pieces.append((kind, width, outs))
        first, after = first + width, outs[0]
    recon = []
    for kind, width, outs in pieces:
        if kind == "x":
            stay, leave = outs
            h = width // 2
            first = move(leave[:, :h], SWAP_X)
            later, first = lax.optimization_barrier((leave[:, h:], first))
            got = jnp.concatenate([first, move(later, SWAP_X)], axis=1)
            total = add(stay, got).astype(BF).reshape(Z, GRP, width)
            recon.append(ring_sum(total[0], total[1], total[3], total[2][:, :h], total[2][:, h:]))
        else:
            total = ring_sum(*outs)
            recon.append(add(total[:GRP], move(total[GRP:].astype(BF), SWAP_X)))
    recon = jnp.concatenate(recon, axis=1)
    target = target_resid[0].astype(F32)
    keep_mask = section_index >= source[:, None]
    result = jnp.where(keep_mask, target - recon, target).astype(BF)
    return result[None]


def solution(mesh):
    placed = (
        P("feat", "section"),
        P(),
        P("section", "feat"),
        P("feat"),
        P("section", "feat", None),
        P("section", "feat", None),
        P(),
        P("feat"),
    )
    return jax.shard_map(
        body, mesh=mesh, in_specs=placed, out_specs=P("section", "feat", None), check_vma=False
    )
```

profile of v0, /device:TPU:0, one launch (start us, length us, event | category | flops | bytes accessed | tf_op | source)
XLA Modules:
  0.0 149.6 jit_solution(13573378673923528013)
XLA Ops:
  0.0 1.1 broadcast_in_dim.20
  1.1 22.3 %all_to_all.25 = bf16[8,64,1024]{2,1,0:T(8,128)(2,1)S(1)} all-to-all(bf16[8,64,1024]{2,1,0:T(8,128)(2,1)S(1)} %broadcast_in_dim.20), channel_id=1, replica_groups={{0,2,4,6,8,10,12,14},{1,3,5,7,9,11,13,15},{16,18,20,22,24,26,28,30},{17..., dimensions={0} | all-to-all | bytes 2097152 | tf_op jit(solution)/shard_map/all_to_all | solution.py:317
  23.6 4.9 %shard_map.82 = (s32[32,1024]{1,0:T(8,128)S(1)}, s32[512,128]{1,0:T(8,128)S(1)}, s32[8,128]{1,0:T(8,128)S(1)}, s32[1,1]{1,0:T(1,128)}) custom-call(s32[2]{0:T(128)S(1)} %pad_add_fusion.where_ref, s32[24,1024]{1,0:T(8,128)S(1)} %bitcast.18, s32[256,1]{1,0:T(8,128)S(1)} %copy.9.slot_ref), custom_call_target="tpu_custom_call" | custom-call | flops 4294967296 | bytes 1048576 | tf_op jit(solution)/shard_map/pallas_call | solution.py:119
  29.1 10.9 %shard_map.83 = bf16[6144,128]{1,0:T(8,128)(2,1)S(1)} custom-call(s32[8,128]{1,0:T(8,128)S(1)} %get-tuple-element.45.meta_ref.after_ref, bf16[512,1024]{1,0:T(8,128)(2,1)S(1)} %bitcast.17, bf16[512,1024]{1,0:T(8,128)(2,1)S(1)} %collective-permute-done.far_ref, s32[32,1024]{1,0:T(8,128)S(1)} %get-tuple-element.48.rows_ref, bf16[1024,2048]{1,0:T(8,128)(2,1)S(1)} %copy-done), custom_call_target="tpu_custom_call" | custom-call | flops 6442450944 | bytes 8388608 | tf_op jit(solution)/shard_map/pallas_call | solution.py:158
  40.0 40.6 %conditional.1 = (bf16[6144,128]{1,0:T(8,128)(2,1)S(1)}) conditional(s32[]{:T(128)} %bitcast.8, (bf16[6144,128]{1,0:T(8,128)(2,1)S(1)}, s32[2]{0:T(128)S(1)}, s32[8,128]{1,0:T(8,128)S(1)}, f32[16,128]{1,0:T(8,128)S(1)}) %tuple.21, (bf16[6144,128]{1,0:T(8,128)(2,1)S(1)}, s32[2]{0:T(128)S(1)}, s32[8,128]{1,0:T(8,128)S(1)}, ...), branch_computations={%region_0.1_spmd, %region_1.2_spmd} | conditional | flops 16777216 | bytes 12255240 | solution.py:331
  40.1 21.0 %all_to_all.23.parts_ref = bf16[8,384,128]{2,1,0:T(8,128)(2,1)S(1)} all-to-all(bf16[8,384,128]{2,1,0:T(8,128)(2,1)S(1)} %bitcast.24), channel_id=1, replica_groups=mesh['section'=8,'feat'=16] {'section'}, dimensions={0} | all-to-all | bytes 1572864 | tf_op jit(solution)/shard_map/cond/branch_1_fun/all_to_all | solution.py:325
  61.1 0.9 branch_1_fun.1
  62.2 18.3 %all_to_all.24 = bf16[8,384,128]{2,1,0:T(8,128)(2,1)S(1)} all-to-all(bf16[8,384,128]{2,1,0:T(8,128)(2,1)S(1)} %broadcast_in_dim.12), channel_id=1, replica_groups=mesh['section'=8,'feat'=16] {'section'}, dimensions={0} | all-to-all | bytes 1572864 | tf_op jit(solution)/shard_map/cond/branch_1_fun/all_to_all | solution.py:328
  80.8 2.8 %shard_map.84.a1_ref = bf16[512,2048]{1,0:T(8,128)(2,1)S(1)} custom-call(s32[8,128]{1,0:T(8,128)S(1)} %get-tuple-element.45.meta_ref.after_ref, s32[512,128]{1,0:T(8,128)S(1)} %get-tuple-element.46.cols_ref, bf16[6144,128]{1,0:T(8,128)(2,1)S(1)} %get-tuple-element.66.act_ref), custom_call_target="tpu_custom_call" | custom-call | flops 1073741824 | bytes 4194304 | tf_op jit(solution)/shard_map/pallas_call | solution.py:227
  83.6 0.6 collective-permute-done.1.act_ref
  84.2 3.5 %shard_map.85.a2_ref = bf16[512,2048]{1,0:T(8,128)(2,1)S(1)} custom-call(s32[8,128]{1,0:T(8,128)S(1)} %get-tuple-element.45.meta_ref.after_ref, s32[512,128]{1,0:T(8,128)S(1)} %get-tuple-element.46.cols_ref, bf16[6144,128]{1,0:T(8,128)(2,1)S(1)} %collective-permute-done.1.act_ref), custom_call_target="tpu_custom_call" | custom-call | flops 1073741824 | bytes 4194304 | tf_op jit(solution)/shard_map/pallas_call | solution.py:227
  87.6 11.7 %shard_map.86 = (bf16[256,2048]{1,0:T(8,128)(2,1)S(1)}, bf16[256,2048]{1,0:T(8,128)(2,1)S(1)}) custom-call(bf16[512,2048]{1,0:T(8,128)(2,1)S(1)} %shard_map.84.a1_ref, bf16[512,2048]{1,0:T(8,128)(2,1)S(1)} %shard_map.85.a2_ref, bf16[2048,4096]{1,0:T(8,128)(2,1)} %bitcast.20, bf16[2048,4096]{1,0:T(8,128)(2,1)} %collective-permute-done.2.w2_ref, ...), custom_call_target="tpu_custom_call" | custom-call | flops 8589934592 | bytes 23068672 | tf_op jit(solution)/shard_map/pallas_call | solution.py:273
  99.5 12.0 %shard_map.87 = (bf16[128,2048]{1,0:T(8,128)(2,1)S(1)}, bf16[128,2048]{1,0:T(8,128)(2,1)S(1)}, bf16[128,2048]{1,0:T(8,128)(2,1)S(1)}, bf16[128,1024]{1,0:T(8,128)(2,1)S(1)}, bf16[128,1024]{1,0:T(8,128)(2,1)S(1)}) custom-call(bf16[512,2048]{1,0:T(8,128)(2,1)S(1)} %shard_map.84.a1_ref, bf16[512,2048]{1,0:T(8,128)(2,1)S(1)} %shard_map.85.a2_ref, ...), custom_call_target="tpu_custom_call" | custom-call | flops 8589934592 | bytes 23068672 | tf_op jit(solution)/shard_map/pallas_call | solution.py:273
  111.7 3.3 %collective-permute-start.11 = (bf16[128,1024]{1,0:T(8,128)(2,1)S(1)}, bf16[128,1024]{1,0:T(8,128)(2,1)S(1)}, u32[]{:S(2)}, u32[]{:S(2)}) collective-permute-start(bf16[128,1024]{1,0:T(8,128)(2,1)S(1)} %get-tuple-element.57), channel_id=1, source_target_pairs={{0,6},{1,7},{2,0},{3,1},{4,2},{5,3},{6,4},{7,5},{8,14},{9,15},{10,... | collective-permute-start | bytes 786440 | tf_op jit(solution)/shard_map/ppermute | solution.py:47
  114.9 6.0 %collective-permute-done.9 = bf16[128,1024]{1,0:T(8,128)(2,1)S(1)} collective-permute-done((bf16[128,1024]{1,0:T(8,128)(2,1)S(1)}, bf16[128,1024]{1,0:T(8,128)(2,1)S(1)}, u32[]{:S(2)}, u32[]{:S(2)}) %collective-permute-start.9) | collective-permute-done | bytes 262176 | tf_op jit(solution)/shard_map/ppermute | solution.py:47
  121.0 1.8 %collective-permute-start.4 = (bf16[256,1024]{1,0:T(8,128)(2,1)S(1)}, bf16[256,1024]{1,0:T(8,128)(2,1)S(1)}, u32[]{:S(2)}, u32[]{:S(2)}) collective-permute-start(bf16[256,1024]{1,0:T(8,128)(2,1)S(1)} %get-tuple-element.52), channel_id=1, source_target_pairs={{0,8},{1,9},{2,10},{3,11},{4,12},{5,13},{6,14},{7,15},{8,0},{9,1},... | collective-permute-start | bytes 1572872 | tf_op jit(solution)/shard_map/ppermute | solution.py:47
  123.1 3.3 %collective-permute-start.12 = (bf16[128,2048]{1,0:T(8,128)(2,1)S(1)}, bf16[128,2048]{1,0:T(8,128)(2,1)S(1)}, u32[]{:S(2)}, u32[]{:S(2)}) collective-permute-start(bf16[128,2048]{1,0:T(8,128)(2,1)S(1)} %pad_maximum_fusion.1), channel_id=1, source_target_pairs={{0,6},{1,7},{2,0},{3,1},{4,2},{5,3},{6,4},{7,5},{8,14},{9,15},{10,... | collective-permute-start | bytes 1572872 | tf_op jit(solution)/shard_map/ppermute | solution.py:47
  126.3 7.7 %collective-permute-done.4 = bf16[256,1024]{1,0:T(8,128)(2,1)S(1)} collective-permute-done((bf16[256,1024]{1,0:T(8,128)(2,1)S(1)}, bf16[256,1024]{1,0:T(8,128)(2,1)S(1)}, u32[]{:S(2)}, u32[]{:S(2)}) %collective-permute-start.4) | collective-permute-done | bytes 524320 | tf_op jit(solution)/shard_map/ppermute | solution.py:47
  134.5 3.2 %collective-permute-start.7 = (bf16[64,1024]{1,0:T(8,128)(2,1)S(1)}, bf16[64,1024]{1,0:T(8,128)(2,1)S(1)}, u32[]{:S(2)}, u32[]{:S(2)}) collective-permute-start(bf16[64,1024]{1,0:T(8,128)(2,1)S(1)} %get-tuple-element.61), channel_id=1, source_target_pairs={{0,6},{1,7},{2,0},{3,1},{4,2},{5,3},{6,4},{7,5},{8,14},{9,15},{10,... | collective-permute-start | bytes 393224 | tf_op jit(solution)/shard_map/ppermute | solution.py:47
  138.0 1.5 collective-permute-start.13
  139.5 1.2 collective-permute-done.5
  140.9 3.3 %collective-permute-start.8 = (bf16[64,2048]{1,0:T(8,128)(2,1)S(1)}, bf16[64,2048]{1,0:T(8,128)(2,1)S(1)}, u32[]{:S(2)}, u32[]{:S(2)}) collective-permute-start(bf16[64,2048]{1,0:T(8,128)(2,1)S(1)} %pad_maximum_fusion.3), channel_id=1, source_target_pairs={{0,6},{1,7},{2,0},{3,1},{4,2},{5,3},{6,4},{7,5},{8,14},{9,15},{10,... | collective-permute-start | bytes 786440 | tf_op jit(solution)/shard_map/ppermute | solution.py:47
  144.5 3.9 %collective-permute-done.6 = bf16[64,2048]{1,0:T(8,128)(2,1)S(1)} collective-permute-done((bf16[64,2048]{1,0:T(8,128)(2,1)S(1)}, bf16[64,2048]{1,0:T(8,128)(2,1)S(1)}, u32[]{:S(2)}, u32[]{:S(2)}) %collective-permute-start.6) | collective-permute-done | bytes 262176 | tf_op jit(solution)/shard_map/ppermute | solution.py:47
  148.6 1.0 fusion
  (51 shorter events, 2.6 us)
Async XLA Ops:
  0.0 23.4 %copy-start.4 = (s32[256]{0:T(256)S(1)}, s32[256]{0:T(256)}, u32[]{:S(2)}) copy-start(s32[256]{0:T(256)} %param.16) | copy-start | bytes 3076
  0.0 23.6 %copy-start.1 = (s32[1024,24]{0,1:T(8,128)S(1)}, s32[1024,24]{0,1:T(8,128)}, u32[]{:S(2)}) copy-start(s32[1024,24]{0,1:T(8,128)} %param.11) | copy-start | bytes 294916
  0.0 87.6 %collective-permute-start.2 = (bf16[2048,4096]{1,0:T(8,128)(2,1)}, bf16[2048,4096]{1,0:T(8,128)(2,1)}, u32[]{:S(2)}, u32[]{:S(2)}) collective-permute-start(bf16[2048,4096]{1,0:T(8,128)(2,1)} %bitcast.19), channel_id=1, source_target_pairs={{0,1},{1,0},{2,3},{3,2},{4,5},{5,4},{6,7},{7,6},{8,9},{9,8},{10,11... | collective-permute-start | bytes 50331656 | tf_op jit(solution)/shard_map/ppermute | solution.py:47
  23.4 5.7 %collective-permute-start = (bf16[512,1024]{1,0:T(8,128)(2,1)S(1)}, bf16[512,1024]{1,0:T(8,128)(2,1)S(1)}, u32[]{:S(2)}, u32[]{:S(2)}) collective-permute-start(bf16[512,1024]{1,0:T(8,128)(2,1)S(1)} %bitcast.16), channel_id=1, source_target_pairs={{0,1},{1,0},{2,3},{3,2},{4,5},{5,4},{6,7},{7,6},{8,9},{9,8},{10,11... | collective-permute-start | bytes 3145736 | tf_op jit(solution)/shard_map/ppermute | solution.py:47
  23.6 5.5 %copy-start = (bf16[1024,2048]{1,0:T(8,128)(2,1)S(1)}, bf16[1024,2048]{1,0:T(8,128)(2,1)}, u32[]{:S(2)}) copy-start(bf16[1024,2048]{1,0:T(8,128)(2,1)} %enc_ref.1) | copy-start | bytes 12582916
  29.1 11.0 %copy-start.3 = (f32[2048]{0:T(1024)S(1)}, f32[2048]{0:T(1024)}, u32[]{:S(2)}) copy-start(f32[2048]{0:T(1024)} %param.13) | copy-start | bytes 24580
  80.7 3.5 %collective-permute-start.1 = (bf16[6144,128]{1,0:T(8,128)(2,1)S(1)}, bf16[6144,128]{1,0:T(8,128)(2,1)S(1)}, u32[]{:S(2)}, u32[]{:S(2)}) collective-permute-start(bf16[6144,128]{1,0:T(8,128)(2,1)S(1)} %get-tuple-element.66.act_ref), channel_id=1, source_target_pairs={{0,1},{1,0},{2,3},{3,2},{4,5},{5,4},{6,7},{7,6},{8,9},{9,8},{10,11... | collective-permute-start | bytes 4718600 | tf_op jit(solution)/shard_map/ppermute | solution.py:47
  99.4 21.6 %collective-permute-start.3 = (bf16[256,1024]{1,0:T(8,128)(2,1)S(1)}, bf16[256,1024]{1,0:T(8,128)(2,1)S(1)}, u32[]{:S(2)}, u32[]{:S(2)}) collective-permute-start(bf16[256,1024]{1,0:T(8,128)(2,1)S(1)} %get-tuple-element.64), channel_id=1, source_target_pairs={{0,8},{1,9},{2,10},{3,11},{4,12},{5,13},{6,14},{7,15},{8,0},{9,1},... | collective-permute-start | bytes 1572872 | tf_op jit(solution)/shard_map/ppermute | solution.py:47
  99.5 12.1 %copy-start.5 = (s32[64]{0:T(128)S(1)}, s32[64]{0:T(128)}, u32[]{:S(2)}) copy-start(s32[64]{0:T(128)} %param.17) | copy-start | bytes 772
  111.5 9.4 %collective-permute-start.9 = (bf16[128,1024]{1,0:T(8,128)(2,1)S(1)}, bf16[128,1024]{1,0:T(8,128)(2,1)S(1)}, u32[]{:S(2)}, u32[]{:S(2)}) collective-permute-start(bf16[128,1024]{1,0:T(8,128)(2,1)S(1)} %get-tuple-element.55), channel_id=1, source_target_pairs={{0,2},{1,3},{2,4},{3,5},{4,6},{5,7},{6,0},{7,1},{8,10},{9,11},{10,... | collective-permute-start | bytes 786440 | tf_op jit(solution)/shard_map/ppermute | solution.py:47
  111.7 11.3 %collective-permute-start.11 = (bf16[128,1024]{1,0:T(8,128)(2,1)S(1)}, bf16[128,1024]{1,0:T(8,128)(2,1)S(1)}, u32[]{:S(2)}, u32[]{:S(2)}) collective-permute-start(bf16[128,1024]{1,0:T(8,128)(2,1)S(1)} %get-tuple-element.57), channel_id=1, source_target_pairs={{0,6},{1,7},{2,0},{3,1},{4,2},{5,3},{6,4},{7,5},{8,14},{9,15},{10,... | collective-permute-start | bytes 786440 | tf_op jit(solution)/shard_map/ppermute | solution.py:47
  121.0 13.0 %collective-permute-start.4 = (bf16[256,1024]{1,0:T(8,128)(2,1)S(1)}, bf16[256,1024]{1,0:T(8,128)(2,1)S(1)}, u32[]{:S(2)}, u32[]{:S(2)}) collective-permute-start(bf16[256,1024]{1,0:T(8,128)(2,1)S(1)} %get-tuple-element.52), channel_id=1, source_target_pairs={{0,8},{1,9},{2,10},{3,11},{4,12},{5,13},{6,14},{7,15},{8,0},{9,1},... | collective-permute-start | bytes 1572872 | tf_op jit(solution)/shard_map/ppermute | solution.py:47
  122.8 14.9 %collective-permute-start.10 = (bf16[128,2048]{1,0:T(8,128)(2,1)S(1)}, bf16[128,2048]{1,0:T(8,128)(2,1)S(1)}, u32[]{:S(2)}, u32[]{:S(2)}) collective-permute-start(bf16[128,2048]{1,0:T(8,128)(2,1)S(1)} %pad_maximum_fusion), channel_id=1, source_target_pairs={{0,2},{1,3},{2,4},{3,5},{4,6},{5,7},{6,0},{7,1},{8,10},{9,11},{10,... | collective-permute-start | bytes 1572872 | tf_op jit(solution)/shard_map/ppermute | solution.py:47
  123.1 14.7 %collective-permute-start.12 = (bf16[128,2048]{1,0:T(8,128)(2,1)S(1)}, bf16[128,2048]{1,0:T(8,128)(2,1)S(1)}, u32[]{:S(2)}, u32[]{:S(2)}) collective-permute-start(bf16[128,2048]{1,0:T(8,128)(2,1)S(1)} %pad_maximum_fusion.1), channel_id=1, source_target_pairs={{0,6},{1,7},{2,0},{3,1},{4,2},{5,3},{6,4},{7,5},{8,14},{9,15},{10,... | collective-permute-start | bytes 1572872 | tf_op jit(solution)/shard_map/ppermute | solution.py:47
  134.4 6.2 %collective-permute-start.5 = (bf16[64,1024]{1,0:T(8,128)(2,1)S(1)}, bf16[64,1024]{1,0:T(8,128)(2,1)S(1)}, u32[]{:S(2)}, u32[]{:S(2)}) collective-permute-start(bf16[64,1024]{1,0:T(8,128)(2,1)S(1)} %get-tuple-element.60), channel_id=1, source_target_pairs={{0,2},{1,3},{2,4},{3,5},{4,6},{5,7},{6,0},{7,1},{8,10},{9,11},{10,... | collective-permute-start | bytes 393224 | tf_op jit(solution)/shard_map/ppermute | solution.py:47
  134.5 6.2 %collective-permute-start.7 = (bf16[64,1024]{1,0:T(8,128)(2,1)S(1)}, bf16[64,1024]{1,0:T(8,128)(2,1)S(1)}, u32[]{:S(2)}, u32[]{:S(2)}) collective-permute-start(bf16[64,1024]{1,0:T(8,128)(2,1)S(1)} %get-tuple-element.61), channel_id=1, source_target_pairs={{0,6},{1,7},{2,0},{3,1},{4,2},{5,3},{6,4},{7,5},{8,14},{9,15},{10,... | collective-permute-start | bytes 393224 | tf_op jit(solution)/shard_map/ppermute | solution.py:47
  138.0 10.5 %copy-start.2 = (bf16[1,64,4096]{2,1,0:T(8,128)(2,1)S(1)}, bf16[1,64,4096]{2,1,0:T(8,128)(2,1)}, u32[]{:S(2)}) copy-start(bf16[1,64,4096]{2,1,0:T(8,128)(2,1)} %param.15) | copy-start | bytes 1572868
  138.0 6.5 %collective-permute-start.13 = (bf16[64,2048]{1,0:T(8,128)(2,1)S(1)}, bf16[64,2048]{1,0:T(8,128)(2,1)S(1)}, u32[]{:S(2)}, u32[]{:S(2)}) collective-permute-start(bf16[64,2048]{1,0:T(8,128)(2,1)S(1)} %slice.96), channel_id=1, source_target_pairs={{0,8},{1,9},{2,10},{3,11},{4,12},{5,13},{6,14},{7,15},{8,0},{9,1},... | collective-permute-start | bytes 786440 | tf_op jit(solution)/shard_map/ppermute | solution.py:47
  140.8 7.7 %collective-permute-start.6 = (bf16[64,2048]{1,0:T(8,128)(2,1)S(1)}, bf16[64,2048]{1,0:T(8,128)(2,1)S(1)}, u32[]{:S(2)}, u32[]{:S(2)}) collective-permute-start(bf16[64,2048]{1,0:T(8,128)(2,1)S(1)} %pad_maximum_fusion.2), channel_id=1, source_target_pairs={{0,2},{1,3},{2,4},{3,5},{4,6},{5,7},{6,0},{7,1},{8,10},{9,11},{10,... | collective-permute-start | bytes 786440 | tf_op jit(solution)/shard_map/ppermute | solution.py:47
  140.9 7.5 %collective-permute-start.8 = (bf16[64,2048]{1,0:T(8,128)(2,1)S(1)}, bf16[64,2048]{1,0:T(8,128)(2,1)S(1)}, u32[]{:S(2)}, u32[]{:S(2)}) collective-permute-start(bf16[64,2048]{1,0:T(8,128)(2,1)S(1)} %pad_maximum_fusion.3), channel_id=1, source_target_pairs={{0,6},{1,7},{2,0},{3,1},{4,2},{5,3},{6,4},{7,5},{8,14},{9,15},{10,... | collective-permute-start | bytes 786440 | tf_op jit(solution)/shard_map/ppermute | solution.py:47
where the time goes:
time: 149 us; the launch traced here: 150 us
  blocking collectives  61.6 us (41%)
  Pallas kernels  46.7 us (31%)
  waiting for transfers between devices  19.7 us (13%)
  starting transfers between devices  16.8 us (11%)
  other arithmetic  2.16 us (1%)
  local copies, waits for them, and re-layouts  1.7 us (1%)
    pallas_call x2, Pallas kernels, decode_call(): pl.pallas_call(functools.partial(decode_kernel, kind, half), grid=(steps,...  23.7 us
    all_to_all x1, blocking collectives, body(): near = lax.all_to_all(copies, 'feat', 0, 0, axis_index_groups=SAME_C)  22.3 us
    all_to_all x1, blocking collectives, exchange(): parts = lax.all_to_all(parts, 'section', 0, 0)  21 us
    ppermute x14, waiting for transfers between devices, move(): return lax.ppermute(x, 'feat', pairs)  19.7 us
    all_to_all x1, blocking collectives, exchange(): act = lax.all_to_all(wide, 'section', 0, 0).reshape(room, BLK)  18.3 us
    ppermute x14, starting transfers between devices, move(): return lax.ppermute(x, 'feat', pairs)  16.8 us
    pallas_call x1, Pallas kernels, encode_call(): pl.pallas_call(encode_kernel, grid=(OWN // 2,), in_specs=[SM, pl.BlockSpe...  10.9 us
    pallas_call x2, Pallas kernels, spread_call(): pl.pallas_call(functools.partial(spread_kernel, first), in_specs=[SM, VM,...  6.28 us
  transfers between devices with their start and end apart: 14, of which 6 were waited for; matrix products, arithmetic and copies ran while one was open for 2% of the time, Pallas kernels for 23%

commit v1 on v0

--- a/solution.py
+++ b/solution.py
@@ -14,8 +14,10 @@
 NPOS = 256
 OWN = 16
 FULL = OWN * CAP
-SMALL = FULL // 2
+ROOMS = (2560, 3072, FULL)
 WIN = 128
+STEP = 8
+EARLY = 768
 HALF = 512
 XL, Z, C = 2, 4, 2
 BF = jnp.bfloat16
@@ -40,7 +42,11 @@
 DOWN = feat_perm(lambda xl, z, c: (xl, (z + Z - 1) % Z, c))
 SWAP_X = feat_perm(lambda xl, z, c: (1 - xl, z, c))
 SWAP_C = feat_perm(lambda xl, z, c: (xl, z, 1 - c))
-SAME_C = [[(xl * Z + z) * C + c for xl in range(XL) for z in range(Z)] for c in range(C)]
+OTHERS = ((0, 1), (0, 3), (1, 0), (0, 2), (1, 1), (1, 3), (1, 2))
+
+
+def chip(dx, dz, xl, z, c):
+    return (xl + dx) % XL, (z + dz) % Z, c
 
 
 def move(x, pairs):
@@ -132,47 +138,66 @@
     )(where, active, slots)
 
 
-def encode_kernel(meta_ref, near_ref, far_ref, rows_ref, enc_ref, out_ref, held):
-    first = pl.program_id(0) * 2
-
-    def pack(b, w):
-        at = pl.multiple_of(meta_ref[0, first + b] + w * WIN, 16)
+def gather_kernel(where_ref, *refs):
+    f = where_ref[0]
+    xl, z = f // (Z * C), (f // C) % Z
+    for (dx, dz), ref in zip(((0, 0),) + OTHERS, refs):
+        g = (xl + XL - dx) % XL * Z + (z + Z - dz) % Z
+        refs[-1][pl.ds(pl.multiple_of(g * GRP, GRP), GRP), :] = ref[...]
+
+
+def gather_call(where, groups, after):
+    return pl.pallas_call(
+        gather_kernel,
+        in_specs=[SM] + [VM] * len(groups) + [ANY],
+        out_specs=VM,
+        out_shape=jax.ShapeDtypeStruct((HALF, groups[0].shape[1]), BF),
+        compiler_params=pltpu.CompilerParams(vmem_limit_bytes=32 << 20),
+        cost_estimate=pl.CostEstimate(flops=0, bytes_accessed=2 << 20, transcendentals=0),
+    )(where, *groups, after)
+
+
+def encode_kernel(meta_ref, half_ref, far_ref, rows_ref, enc_ref, out_ref, held):
+    first = pl.program_id(0) * STEP
+
+    def pack(b, skip, size):
+        at = pl.multiple_of(meta_ref[0, first + b] + skip, 16)
         place = rows_ref[pl.ds(first + b, 1), :]
-        one = jnp.where(iota((WIN, TOK), 0) == place - at, 1.0, 0.0).astype(BF)
+        one = jnp.where(iota((size, TOK), 0) == place - at, 1.0, 0.0).astype(BF)
         part = held[:, b * BLK : (b + 1) * BLK]
-        out_ref[pl.ds(at, WIN), :] = jnp.dot(one, part, preferred_element_type=F32).astype(BF)
-
-    enc = enc_ref[...]
-    held[:HALF, :] = jnp.dot(near_ref[...], enc, preferred_element_type=F32).astype(BF)
-    held[HALF:, :] = jnp.dot(far_ref[...], enc, preferred_element_type=F32).astype(BF)
-    for b in range(2):
-        pack(b, 0)
-        for w in range(1, CAP // WIN):
-
-            @pl.when(meta_ref[0, 2 * OWN + first + b] > w * WIN)
-            def _(b=b, w=w):
-                pack(b, w)
-
-
-def encode_call(meta, near, far, rows, enc):
+        out_ref[pl.ds(at, size), :] = jnp.dot(one, part, preferred_element_type=F32).astype(BF)
+
+    held[:HALF, :] = half_ref[...]
+    held[HALF:, :] = jnp.dot(
+        far_ref[...], enc_ref[...], preferred_element_type=F32
+    ).astype(BF)
+    for b in range(STEP):
+        pack(b, 0, WIN)
+
+        @pl.when(meta_ref[0, 2 * OWN + first + b] > WIN)
+        def _(b=b):
+            pack(b, WIN, CAP - WIN)
+
+
+def encode_call(meta, half, far, rows, enc):
     return pl.pallas_call(
         encode_kernel,
-        grid=(OWN // 2,),
+        grid=(OWN // STEP,),
         in_specs=[
             SM,
-            pl.BlockSpec(near.shape, lambda i: (0, 0)),
+            pl.BlockSpec((HALF, STEP * BLK), lambda i: (0, i)),
             pl.BlockSpec(far.shape, lambda i: (0, 0)),
             pl.BlockSpec((2 * OWN, TOK), lambda i: (0, 0)),
-            pl.BlockSpec((enc.shape[0], 2 * BLK), lambda i: (0, i)),
+            pl.BlockSpec((enc.shape[0], STEP * BLK), lambda i: (0, i)),
         ],
         out_specs=pl.BlockSpec((FULL, BLK), lambda i: (0, 0)),
         out_shape=jax.ShapeDtypeStruct((FULL, BLK), BF),
-        scratch_shapes=[pltpu.VMEM((TOK, 2 * BLK), BF)],
+        scratch_shapes=[pltpu.VMEM((TOK, STEP * BLK), BF)],
         compiler_params=pltpu.CompilerParams(
             vmem_limit_bytes=32 << 20, dimension_semantics=("arbitrary",)
         ),
-        cost_estimate=pl.CostEstimate(flops=6 << 30, bytes_accessed=8 << 20, transcendentals=0),
-    )(meta, near, far, rows, enc)
+        cost_estimate=pl.CostEstimate(flops=4 << 30, bytes_accessed=8 << 20, transcendentals=0),
+    )(meta, half, far, rows, enc)
 
 
 def reduce_kernel(where_ref, meta_ref, parts_ref, bias_ref, out_ref):
@@ -311,12 +336,14 @@
     sections = lax.axis_size("section")
     where = jnp.stack([feat_index, section_index]).astype(I32)
     decoder = dec_weight[0]
-    other_decoder = move(decoder, SWAP_C)
     rows, cols, meta, most = index_call(where, active.T, slot_block.reshape(NPOS, 1))
-    copies = jnp.broadcast_to(resid_in[None], (XL * Z,) + resid_in.shape)
-    near = lax.all_to_all(copies, "feat", 0, 0, axis_index_groups=SAME_C)
-    near = near.reshape(HALF, resid_in.shape[1])
-    packed = encode_call(meta, near, move(near, SWAP_C), rows, enc_weight)
+    near = [resid_in] + [move(resid_in, feat_perm(functools.partial(chip, *o))) for o in OTHERS]
+    near = gather_call(where, near, meta)
+    far = move(near, SWAP_C)
+    leaving, far = lax.optimization_barrier((decoder, far))
+    other_decoder = move(leaving, SWAP_C)
+    half = jnp.dot(near, enc_weight, preferred_element_type=F32).astype(BF)
+    packed = encode_call(meta, half, far, rows, enc_weight)
     bias = enc_bias.reshape(OWN, BLK)
 
     def exchange(room, packed):
@@ -328,10 +355,9 @@
         act = lax.all_to_all(wide, "section", 0, 0).reshape(room, BLK)
         return jnp.pad(act, ((0, FULL - room), (0, 0)))
 
-    act = lax.cond(
-        most[0, 0] <= SMALL,
-        functools.partial(exchange, SMALL),
-        functools.partial(exchange, FULL),
+    act = lax.switch(
+        sum((most[0, 0] > room).astype(I32) for room in ROOMS[:-1]),
+        [functools.partial(exchange, room) for room in ROOMS],
         packed,
     )
     theirs = move(act, SWAP_C)
@@ -341,18 +367,21 @@
     pieces, first, after = [], 0, meta
     for kind, width in PLAN:
         outs = decode_call(kind, own, theirs, decoder, other_decoder, first, width, after)
-        pieces.append((kind, width, outs))
+        pieces.append((kind, width, list(outs)))
         first, after = first + width, outs[0]
     recon = []
     for kind, width, outs in pieces:
         if kind == "x":
             stay, leave = outs
-            h = width // 2
-            first = move(leave[:, :h], SWAP_X)
-            later, first = lax.optimization_barrier((leave[:, h:], first))
+            first = move(leave[:, :EARLY], SWAP_X)
+            later, first, left, right = lax.optimization_barrier(
+                (leave[:, EARLY:], first, pieces[1][2][3], pieces[1][2][4])
+            )
+            pieces[1][2][3:] = [left, right]
             got = jnp.concatenate([first, move(later, SWAP_X)], axis=1)
             total = add(stay, got).astype(BF).reshape(Z, GRP, width)
-            recon.append(ring_sum(total[0], total[1], total[3], total[2][:, :h], total[2][:, h:]))
+            steps = [feat_perm(functools.partial(chip, 0, k)) for k in range(1, Z)]
+            recon.append(add(total[0], *[move(total[k + 1], steps[k]) for k in range(Z - 1)]))
         else:
             total = ring_sum(*outs)
             recon.append(add(total[:GRP], move(total[GRP:].astype(BF), SWAP_X)))

time: 149 us -> 144 us (0.966); the launches traced: 150 us -> 142 us
  blocking collectives: 61.6 us -> 33.6 us
  waiting for transfers between devices: 19.7 us -> 29.7 us
  starting transfers between devices: 16.8 us -> 26.7 us
  Pallas kernels: 46.7 us -> 43.1 us
  matrix products: 0 us -> 2.34 us
    all_to_all x1 -> x0, blocking collectives: 22.3 us -> none  [body(): near = lax.all_to_all(copies, 'feat', 0, 0, axis_index_groups=SAME_C)]
    ppermute x14 -> x20, waiting for transfers between devices: 19.7 us -> 29.7 us  [move(): return lax.ppermute(x, 'feat', pairs)]
    ppermute x14 -> x20, starting transfers between devices: 16.8 us -> 26.7 us  [move(): return lax.ppermute(x, 'feat', pairs)]
    all_to_all x1, blocking collectives: 18.3 us -> 14.6 us  [exchange(): act = lax.all_to_all(wide, 'section', 0, 0).reshape(room, BLK)]
    pallas_call x1 -> x2, Pallas kernels: 10.9 us -> 8.52 us  [the longest x1 7.88 us: encode_call(): pl.pallas_call(encode_kernel, grid=(OWN // STEP,), in_specs=[SM, pl.Block...]
    dot_general x0 -> x1, matrix products: none -> 2.34 us  [body(): half = jnp.dot(near, enc_weight, preferred_element_type=F32).astype(BF)]
    all_to_all x1, blocking collectives: 21 us -> 19 us  [exchange(): parts = lax.all_to_all(parts, 'section', 0, 0)]
  transfers between devices with their start and end apart: 14 -> 20, of which waited for: 6 -> 8; matrix products, arithmetic and copies ran while one was open for 2% -> 3% of each run, Pallas kernels for 23% -> 22%
where the time goes in v1:
time: 144 us; the launch traced here: 142 us
  Pallas kernels  43.1 us (30%)
  blocking collectives  33.6 us (23%)
  waiting for transfers between devices  29.7 us (21%)
  starting transfers between devices  26.7 us (19%)
  matrix products  2.34 us (2%)
  local copies, waits for them, and re-layouts  2.22 us (2%)
  other arithmetic  2.01 us (1%)
  between operations  1.71 us (1%)
    ppermute x20, waiting for transfers between devices, move(): return lax.ppermute(x, 'feat', pairs)  29.7 us
    ppermute x20, starting transfers between devices, move(): return lax.ppermute(x, 'feat', pairs)  26.7 us
    pallas_call x2, Pallas kernels, decode_call(): pl.pallas_call(functools.partial(decode_kernel, kind, half), grid=(steps,...  23.7 us
    all_to_all x1, blocking collectives, exchange(): parts = lax.all_to_all(parts, 'section', 0, 0)  19 us
    all_to_all x1, blocking collectives, exchange(): act = lax.all_to_all(wide, 'section', 0, 0).reshape(room, BLK)  14.6 us
    pallas_call x1, Pallas kernels, encode_call(): pl.pallas_call(encode_kernel, grid=(OWN // STEP,), in_specs=[SM, pl.Block...  7.88 us
    pallas_call x2, Pallas kernels, spread_call(): pl.pallas_call(functools.partial(spread_kernel, first), in_specs=[SM, VM,...  5.21 us
    pallas_call x1, Pallas kernels, index_call(): pl.pallas_call(index_kernel, in_specs=[SM, VM, VM], out_specs=[VM, VM, VM...  4.86 us
  transfers between devices with their start and end apart: 20, of which 8 were waited for; matrix products, arithmetic and copies ran while one was open for 3% of the time, Pallas kernels for 22%

profile of v1, /device:TPU:0, one launch (start us, length us, event | category | flops | bytes accessed | tf_op | source)
XLA Modules:
  0.0 141.5 jit_solution(9840329311025040973)
XLA Ops:
  0.0 5.0 %collective-permute-start.5 = (bf16[64,1024]{1,0:T(8,128)(2,1)}, bf16[64,1024]{1,0:T(8,128)(2,1)S(1)}, u32[]{:S(2)}, u32[]{:S(2)}) collective-permute-start(bf16[64,1024]{1,0:T(8,128)(2,1)} %refs_0_.1), channel_id=1, source_target_pairs={{0,14},{1,15},{2,8},{3,9},{4,10},{5,11},{6,12},{7,13},{8,6},{9,7},... | collective-permute-start | bytes 393224 | tf_op jit(solution)/shard_map/ppermute | solution.py:53
  5.1 1.8 %collective-permute-start.3 = (bf16[64,1024]{1,0:T(8,128)(2,1)}, bf16[64,1024]{1,0:T(8,128)(2,1)S(1)}, u32[]{:S(2)}, u32[]{:S(2)}) collective-permute-start(bf16[64,1024]{1,0:T(8,128)(2,1)} %refs_0_.1), channel_id=1, source_target_pairs={{0,4},{1,5},{2,6},{3,7},{4,0},{5,1},{6,2},{7,3},{8,12},{9,13},{10,... | collective-permute-start | bytes 393224 | tf_op jit(solution)/shard_map/ppermute | solution.py:53
  6.9 1.5 %collective-permute-start.2 = (bf16[64,1024]{1,0:T(8,128)(2,1)}, bf16[64,1024]{1,0:T(8,128)(2,1)S(1)}, u32[]{:S(2)}, u32[]{:S(2)}) collective-permute-start(bf16[64,1024]{1,0:T(8,128)(2,1)} %refs_0_.1), channel_id=1, source_target_pairs={{0,8},{1,9},{2,10},{3,11},{4,12},{5,13},{6,14},{7,15},{8,0},{9,1},... | collective-permute-start | bytes 393224 | tf_op jit(solution)/shard_map/ppermute | solution.py:53
  11.5 3.0 %collective-permute-done.4.refs_5_ = bf16[64,1024]{1,0:T(8,128)(2,1)S(1)} collective-permute-done((bf16[64,1024]{1,0:T(8,128)(2,1)}, bf16[64,1024]{1,0:T(8,128)(2,1)S(1)}, u32[]{:S(2)}, u32[]{:S(2)}) %collective-permute-start.4) | collective-permute-done | bytes 131104 | tf_op jit(solution)/shard_map/ppermute | solution.py:53
  16.7 4.9 %shard_map.82 = (s32[32,1024]{1,0:T(8,128)S(1)}, s32[512,128]{1,0:T(8,128)S(1)}, s32[8,128]{1,0:T(8,128)S(1)}, s32[1,1]{1,0:T(1,128)}) custom-call(s32[2]{0:T(128)S(1)} %pad_add_fusion.where_ref, s32[24,1024]{1,0:T(8,128)S(1)} %bitcast.19, s32[256,1]{1,0:T(8,128)S(1)} %copy.9.slot_ref), custom_call_target="tpu_custom_call" | custom-call | flops 4294967296 | bytes 1048576 | tf_op jit(solution)/shard_map/pallas_call | solution.py:125
  22.8 2.6 %collective-permute-done.7.far_ref = bf16[512,1024]{1,0:T(8,128)(2,1)S(1)} collective-permute-done((bf16[512,1024]{1,0:T(8,128)(2,1)S(1)}, bf16[512,1024]{1,0:T(8,128)(2,1)S(1)}, u32[]{:S(2)}, u32[]{:S(2)}) %collective-permute-start.7) | collective-permute-done | bytes 1048608 | tf_op jit(solution)/shard_map/ppermute | solution.py:53
  27.0 2.3 %convolution_convert_fusion.half_ref = bf16[512,2048]{1,0:T(8,128)(2,1)S(1)} fusion(bf16[512,1024]{1,0:T(8,128)(2,1)S(1)} %shard_map.83, bf16[1024,2048]{1,0:T(8,128)(2,1)S(1)} %copy-done.1), kind=kOutput, calls=%fused_computation | convolution fusion | flops 2148532224 | bytes 7340032 | tf_op jit(solution)/shard_map/dot_general | solution.py:345
  29.3 7.9 %shard_map.84 = bf16[6144,128]{1,0:T(8,128)(2,1)S(1)} custom-call(s32[8,128]{1,0:T(8,128)S(1)} %get-tuple-element.62.refs_8_.meta_ref.after_ref, bf16[512,2048]{1,0:T(8,128)(2,1)S(1)} %convolution_convert_fusion.half_ref, bf16[512,1024]{1,0:T(8,128)(2,1)S(1)} %collective-permute-done.7.far_ref, s32[32,1024]{1,0:T(8,128)S(1)} %get-tuple-element.66.rows_ref, ...), custom_call_target="tpu_custom_call" | custom-call | flops 4294967296 | bytes 8388608 | tf_op jit(solution)/shard_map/pallas_call | solution.py:183
  37.2 34.8 %conditional.1 = (bf16[6144,128]{1,0:T(8,128)(2,1)S(1)}) conditional(s32[]{:T(128)} %bitcast.10, (bf16[6144,128]{1,0:T(8,128)(2,1)S(1)}, s32[2]{0:T(128)S(1)}, s32[8,128]{1,0:T(8,128)S(1)}, f32[16,128]{1,0:T(8,128)S(1)}) %tuple.24, (bf16[6144,128]{1,0:T(8,128)(2,1)S(1)}, s32[2]{0:T(128)S(1)}, s32[8,128]{1,0:T(8,128)S(1)}, ...), branch_computations={%region_0.1_spmd, %region_1.2_spmd, %region_2.3_spmd} | conditional | flops 16777216 | bytes 12255240 | solution.py:358
  37.3 19.0 %all_to_all.24.parts_ref = bf16[8,320,128]{2,1,0:T(8,128)(2,1)S(1)} all-to-all(bf16[8,320,128]{2,1,0:T(8,128)(2,1)S(1)} %bitcast.27), channel_id=1, replica_groups=mesh['section'=8,'feat'=16] {'section'}, dimensions={0} | all-to-all | bytes 1310720 | tf_op jit(solution)/shard_map/cond/branch_0_fun/all_to_all | solution.py:352
  57.3 14.6 %all_to_all.25 = bf16[8,320,128]{2,1,0:T(8,128)(2,1)S(1)} all-to-all(bf16[8,320,128]{2,1,0:T(8,128)(2,1)S(1)} %broadcast_in_dim.11), channel_id=1, replica_groups=mesh['section'=8,'feat'=16] {'section'}, dimensions={0} | all-to-all | bytes 1310720 | tf_op jit(solution)/shard_map/cond/branch_0_fun/all_to_all | solution.py:355
  72.2 3.1 %shard_map.85.a1_ref = bf16[512,2048]{1,0:T(8,128)(2,1)S(1)} custom-call(s32[8,128]{1,0:T(8,128)S(1)} %get-tuple-element.62.refs_8_.meta_ref.after_ref, s32[512,128]{1,0:T(8,128)S(1)} %get-tuple-element.63.cols_ref, bf16[6144,128]{1,0:T(8,128)(2,1)S(1)} %get-tuple-element.82.act_ref), custom_call_target="tpu_custom_call" | custom-call | flops 1073741824 | bytes 4194304 | tf_op jit(solution)/shard_map/pallas_call | solution.py:252
  75.6 2.1 %shard_map.86.a2_ref = bf16[512,2048]{1,0:T(8,128)(2,1)S(1)} custom-call(s32[8,128]{1,0:T(8,128)S(1)} %get-tuple-element.62.refs_8_.meta_ref.after_ref, s32[512,128]{1,0:T(8,128)S(1)} %get-tuple-element.63.cols_ref, bf16[6144,128]{1,0:T(8,128)(2,1)S(1)} %collective-permute-done.8.act_ref), custom_call_target="tpu_custom_call" | custom-call | flops 1073741824 | bytes 4194304 | tf_op jit(solution)/shard_map/pallas_call | solution.py:252
  77.7 11.7 %shard_map.87 = (bf16[256,2048]{1,0:T(8,128)(2,1)S(1)}, bf16[256,2048]{1,0:T(8,128)(2,1)S(1)}) custom-call(bf16[512,2048]{1,0:T(8,128)(2,1)S(1)} %shard_map.85.a1_ref, bf16[512,2048]{1,0:T(8,128)(2,1)S(1)} %shard_map.86.a2_ref, bf16[2048,4096]{1,0:T(8,128)(2,1)} %bitcast.21, bf16[2048,4096]{1,0:T(8,128)(2,1)} %collective-permute-done.9.w2_ref, ...), custom_call_target="tpu_custom_call" | custom-call | flops 8589934592 | bytes 23068672 | tf_op jit(solution)/shard_map/pallas_call | solution.py:298
  89.4 1.9 %collective-permute-start.10 = (bf16[256,768]{1,0:T(8,128)(2,1)S(1)}, bf16[256,768]{1,0:T(8,128)(2,1)S(1)}, u32[]{:S(2)}, u32[]{:S(2)}) collective-permute-start(bf16[256,768]{1,0:T(8,128)(2,1)S(1)} %slice.48), channel_id=1, source_target_pairs={{0,8},{1,9},{2,10},{3,11},{4,12},{5,13},{6,14},{7,15},{8,0},{9,1},... | collective-permute-start | bytes 1179656 | tf_op jit(solution)/shard_map/ppermute | solution.py:53
  91.4 12.0 %shard_map.88 = (bf16[128,2048]{1,0:T(8,128)(2,1)S(1)}, bf16[128,2048]{1,0:T(8,128)(2,1)S(1)}, bf16[128,2048]{1,0:T(8,128)(2,1)S(1)}, bf16[128,1024]{1,0:T(8,128)(2,1)S(1)}, bf16[128,1024]{1,0:T(8,128)(2,1)S(1)}) custom-call(bf16[512,2048]{1,0:T(8,128)(2,1)S(1)} %shard_map.85.a1_ref, bf16[512,2048]{1,0:T(8,128)(2,1)S(1)} %shard_map.86.a2_ref, ...), custom_call_target="tpu_custom_call" | custom-call | flops 8589934592 | bytes 23068672 | tf_op jit(solution)/shard_map/pallas_call | solution.py:298
  103.4 3.2 %collective-permute-start.17 = (bf16[128,1024]{1,0:T(8,128)(2,1)S(1)}, bf16[128,1024]{1,0:T(8,128)(2,1)S(1)}, u32[]{:S(2)}, u32[]{:S(2)}) collective-permute-start(bf16[128,1024]{1,0:T(8,128)(2,1)S(1)} %get-tuple-element.78), channel_id=1, source_target_pairs={{0,6},{1,7},{2,0},{3,1},{4,2},{5,3},{6,4},{7,5},{8,14},{9,15},{10,... | collective-permute-start | bytes 786440 | tf_op jit(solution)/shard_map/ppermute | solution.py:53
  106.8 5.0 %collective-permute-done.17 = bf16[128,1024]{1,0:T(8,128)(2,1)S(1)} collective-permute-done((bf16[128,1024]{1,0:T(8,128)(2,1)S(1)}, bf16[128,1024]{1,0:T(8,128)(2,1)S(1)}, u32[]{:S(2)}, u32[]{:S(2)}) %collective-permute-start.17) | collective-permute-done | bytes 262176 | tf_op jit(solution)/shard_map/ppermute | solution.py:53
  111.9 3.7 %collective-permute-start.18 = (bf16[128,2048]{1,0:T(8,128)(2,1)S(1)}, bf16[128,2048]{1,0:T(8,128)(2,1)S(1)}, u32[]{:S(2)}, u32[]{:S(2)}) collective-permute-start(bf16[128,2048]{1,0:T(8,128)(2,1)S(1)} %pad_maximum_fusion.1), channel_id=1, source_target_pairs={{0,6},{1,7},{2,0},{3,1},{4,2},{5,3},{6,4},{7,5},{8,14},{9,15},{10,... | collective-permute-start | bytes 1572872 | tf_op jit(solution)/shard_map/ppermute | solution.py:53
  115.8 6.8 %collective-permute-done.11 = bf16[256,1280]{1,0:T(8,128)(2,1)S(1)} collective-permute-done((bf16[256,1280]{1,0:T(8,128)(2,1)S(1)}, bf16[256,1280]{1,0:T(8,128)(2,1)S(1)}, u32[]{:S(2)}, u32[]{:S(2)}) %collective-permute-start.11) | collective-permute-done | bytes 655392 | tf_op jit(solution)/shard_map/ppermute | solution.py:53
  124.3 1.9 %collective-permute-start.14 = (bf16[64,2048]{1,0:T(8,128)(2,1)S(1)}, bf16[64,2048]{1,0:T(8,128)(2,1)S(1)}, u32[]{:S(2)}, u32[]{:S(2)}) collective-permute-start(bf16[64,2048]{1,0:T(8,128)(2,1)S(1)} %get-tuple-element.80), channel_id=1, source_target_pairs={{0,6},{1,7},{2,0},{3,1},{4,2},{5,3},{6,4},{7,5},{8,14},{9,15},{10,... | collective-permute-start | bytes 786440 | tf_op jit(solution)/shard_map/ppermute | solution.py:53
  126.3 1.9 %collective-permute-start.13 = (bf16[64,2048]{1,0:T(8,128)(2,1)S(1)}, bf16[64,2048]{1,0:T(8,128)(2,1)S(1)}, u32[]{:S(2)}, u32[]{:S(2)}) collective-permute-start(bf16[64,2048]{1,0:T(8,128)(2,1)S(1)} %get-tuple-element.81), channel_id=1, source_target_pairs={{0,4},{1,5},{2,6},{3,7},{4,0},{5,1},{6,2},{7,3},{8,12},{9,13},{10,... | collective-permute-start | bytes 786440 | tf_op jit(solution)/shard_map/ppermute | solution.py:53
  128.1 4.1 %collective-permute-done.16 = bf16[128,2048]{1,0:T(8,128)(2,1)S(1)} collective-permute-done((bf16[128,2048]{1,0:T(8,128)(2,1)S(1)}, bf16[128,2048]{1,0:T(8,128)(2,1)S(1)}, u32[]{:S(2)}, u32[]{:S(2)}) %collective-permute-start.16) | collective-permute-done | bytes 524320 | tf_op jit(solution)/shard_map/ppermute | solution.py:53
  132.7 7.6 %collective-permute-done.12 = bf16[64,2048]{1,0:T(8,128)(2,1)S(1)} collective-permute-done((bf16[64,2048]{1,0:T(8,128)(2,1)S(1)}, bf16[64,2048]{1,0:T(8,128)(2,1)S(1)}, u32[]{:S(2)}, u32[]{:S(2)}) %collective-permute-start.12) | collective-permute-done | bytes 262176 | tf_op jit(solution)/shard_map/ppermute | solution.py:53
  (61 shorter events, 12.3 us)
Async XLA Ops:
  0.0 10.6 %collective-permute-start.5 = (bf16[64,1024]{1,0:T(8,128)(2,1)}, bf16[64,1024]{1,0:T(8,128)(2,1)S(1)}, u32[]{:S(2)}, u32[]{:S(2)}) collective-permute-start(bf16[64,1024]{1,0:T(8,128)(2,1)} %refs_0_.1), channel_id=1, source_target_pairs={{0,14},{1,15},{2,8},{3,9},{4,10},{5,11},{6,12},{7,13},{8,6},{9,7},... | collective-permute-start | bytes 393224 | tf_op jit(solution)/shard_map/ppermute | solution.py:53
  5.0 9.4 %collective-permute-start.4 = (bf16[64,1024]{1,0:T(8,128)(2,1)}, bf16[64,1024]{1,0:T(8,128)(2,1)S(1)}, u32[]{:S(2)}, u32[]{:S(2)}) collective-permute-start(bf16[64,1024]{1,0:T(8,128)(2,1)} %refs_0_.1), channel_id=1, source_target_pairs={{0,10},{1,11},{2,12},{3,13},{4,14},{5,15},{6,8},{7,9},{8,2},{9,3},... | collective-permute-start | bytes 393224 | tf_op jit(solution)/shard_map/ppermute | solution.py:53
  5.1 16.5 %collective-permute-start.3 = (bf16[64,1024]{1,0:T(8,128)(2,1)}, bf16[64,1024]{1,0:T(8,128)(2,1)S(1)}, u32[]{:S(2)}, u32[]{:S(2)}) collective-permute-start(bf16[64,1024]{1,0:T(8,128)(2,1)} %refs_0_.1), channel_id=1, source_target_pairs={{0,4},{1,5},{2,6},{3,7},{4,0},{5,1},{6,2},{7,3},{8,12},{9,13},{10,... | collective-permute-start | bytes 393224 | tf_op jit(solution)/shard_map/ppermute | solution.py:53
  6.9 14.7 %collective-permute-start.2 = (bf16[64,1024]{1,0:T(8,128)(2,1)}, bf16[64,1024]{1,0:T(8,128)(2,1)S(1)}, u32[]{:S(2)}, u32[]{:S(2)}) collective-permute-start(bf16[64,1024]{1,0:T(8,128)(2,1)} %refs_0_.1), channel_id=1, source_target_pairs={{0,8},{1,9},{2,10},{3,11},{4,12},{5,13},{6,14},{7,15},{8,0},{9,1},... | collective-permute-start | bytes 393224 | tf_op jit(solution)/shard_map/ppermute | solution.py:53
  8.4 13.2 %collective-permute-start.1 = (bf16[64,1024]{1,0:T(8,128)(2,1)}, bf16[64,1024]{1,0:T(8,128)(2,1)S(1)}, u32[]{:S(2)}, u32[]{:S(2)}) collective-permute-start(bf16[64,1024]{1,0:T(8,128)(2,1)} %refs_0_.1), channel_id=1, source_target_pairs={{0,6},{1,7},{2,0},{3,1},{4,2},{5,3},{6,4},{7,5},{8,14},{9,15},{10,... | collective-permute-start | bytes 393224 | tf_op jit(solution)/shard_map/ppermute | solution.py:53
  10.6 10.9 %collective-permute-start = (bf16[64,1024]{1,0:T(8,128)(2,1)}, bf16[64,1024]{1,0:T(8,128)(2,1)S(1)}, u32[]{:S(2)}, u32[]{:S(2)}) collective-permute-start(bf16[64,1024]{1,0:T(8,128)(2,1)} %refs_0_.1), channel_id=1, source_target_pairs={{0,2},{1,3},{2,4},{3,5},{4,6},{5,7},{6,0},{7,1},{8,10},{9,11},{10,... | collective-permute-start | bytes 393224 | tf_op jit(solution)/shard_map/ppermute | solution.py:53
  14.5 7.6 %collective-permute-start.6 = (bf16[64,1024]{1,0:T(8,128)(2,1)}, bf16[64,1024]{1,0:T(8,128)(2,1)S(1)}, u32[]{:S(2)}, u32[]{:S(2)}) collective-permute-start(bf16[64,1024]{1,0:T(8,128)(2,1)} %refs_0_.1), channel_id=1, source_target_pairs={{0,12},{1,13},{2,14},{3,15},{4,8},{5,9},{6,10},{7,11},{8,4},{9,5},... | collective-permute-start | bytes 393224 | tf_op jit(solution)/shard_map/ppermute | solution.py:53
  16.7 10.3 %copy-start.1 = (bf16[1024,2048]{1,0:T(8,128)(2,1)S(1)}, bf16[1024,2048]{1,0:T(8,128)(2,1)}, u32[]{:S(2)}) copy-start(bf16[1024,2048]{1,0:T(8,128)(2,1)} %enc_ref.1) | copy-start | bytes 12582916
  22.7 2.7 %collective-permute-start.7 = (bf16[512,1024]{1,0:T(8,128)(2,1)S(1)}, bf16[512,1024]{1,0:T(8,128)(2,1)S(1)}, u32[]{:S(2)}, u32[]{:S(2)}) collective-permute-start(bf16[512,1024]{1,0:T(8,128)(2,1)S(1)} %shard_map.83), channel_id=1, source_target_pairs={{0,1},{1,0},{2,3},{3,2},{4,5},{5,4},{6,7},{7,6},{8,9},{9,8},{10,11... | collective-permute-start | bytes 3145736 | tf_op jit(solution)/shard_map/ppermute | solution.py:53
  25.5 52.2 %collective-permute-start.9 = (bf16[2048,4096]{1,0:T(8,128)(2,1)}, bf16[2048,4096]{1,0:T(8,128)(2,1)}, u32[]{:S(2)}, u32[]{:S(2)}) collective-permute-start(bf16[2048,4096]{1,0:T(8,128)(2,1)} %bitcast.20), channel_id=1, source_target_pairs={{0,1},{1,0},{2,3},{3,2},{4,5},{5,4},{6,7},{7,6},{8,9},{9,8},{10,11... | collective-permute-start | bytes 50331656 | tf_op jit(solution)/shard_map/ppermute | solution.py:53
  29.3 7.9 %copy-start.4 = (f32[2048]{0:T(1024)S(1)}, f32[2048]{0:T(1024)}, u32[]{:S(2)}) copy-start(f32[2048]{0:T(1024)} %param.14) | copy-start | bytes 24580
  72.1 3.5 %collective-permute-start.8 = (bf16[6144,128]{1,0:T(8,128)(2,1)S(1)}, bf16[6144,128]{1,0:T(8,128)(2,1)S(1)}, u32[]{:S(2)}, u32[]{:S(2)}) collective-permute-start(bf16[6144,128]{1,0:T(8,128)(2,1)S(1)} %get-tuple-element.82.act_ref), channel_id=1, source_target_pairs={{0,1},{1,0},{2,3},{3,2},{4,5},{5,4},{6,7},{7,6},{8,9},{9,8},{10,11... | collective-permute-start | bytes 4718600 | tf_op jit(solution)/shard_map/ppermute | solution.py:53
  89.4 13.9 %collective-permute-start.10 = (bf16[256,768]{1,0:T(8,128)(2,1)S(1)}, bf16[256,768]{1,0:T(8,128)(2,1)S(1)}, u32[]{:S(2)}, u32[]{:S(2)}) collective-permute-start(bf16[256,768]{1,0:T(8,128)(2,1)S(1)} %slice.48), channel_id=1, source_target_pairs={{0,8},{1,9},{2,10},{3,11},{4,12},{5,13},{6,14},{7,15},{8,0},{9,1},... | collective-permute-start | bytes 1179656 | tf_op jit(solution)/shard_map/ppermute | solution.py:53
  91.4 15.2 %copy-start.5 = (s32[64]{0:T(128)S(1)}, s32[64]{0:T(128)}, u32[]{:S(2)}) copy-start(s32[64]{0:T(128)} %param.18) | copy-start | bytes 772
  103.4 8.4 %collective-permute-start.17 = (bf16[128,1024]{1,0:T(8,128)(2,1)S(1)}, bf16[128,1024]{1,0:T(8,128)(2,1)S(1)}, u32[]{:S(2)}, u32[]{:S(2)}) collective-permute-start(bf16[128,1024]{1,0:T(8,128)(2,1)S(1)} %get-tuple-element.78), channel_id=1, source_target_pairs={{0,6},{1,7},{2,0},{3,1},{4,2},{5,3},{6,4},{7,5},{8,14},{9,15},{10,... | collective-permute-start | bytes 786440 | tf_op jit(solution)/shard_map/ppermute | solution.py:53
  106.6 9.0 %collective-permute-start.15 = (bf16[128,1024]{1,0:T(8,128)(2,1)S(1)}, bf16[128,1024]{1,0:T(8,128)(2,1)S(1)}, u32[]{:S(2)}, u32[]{:S(2)}) collective-permute-start(bf16[128,1024]{1,0:T(8,128)(2,1)S(1)} %get-tuple-element.76), channel_id=1, source_target_pairs={{0,2},{1,3},{2,4},{3,5},{4,6},{5,7},{6,0},{7,1},{8,10},{9,11},{10,... | collective-permute-start | bytes 786440 | tf_op jit(solution)/shard_map/ppermute | solution.py:53
  106.7 15.9 %collective-permute-start.11 = (bf16[256,1280]{1,0:T(8,128)(2,1)S(1)}, bf16[256,1280]{1,0:T(8,128)(2,1)S(1)}, u32[]{:S(2)}, u32[]{:S(2)}) collective-permute-start(bf16[256,1280]{1,0:T(8,128)(2,1)S(1)} %slice.47), channel_id=1, source_target_pairs={{0,8},{1,9},{2,10},{3,11},{4,12},{5,13},{6,14},{7,15},{8,0},{9,1},... | collective-permute-start | bytes 1966088 | tf_op jit(solution)/shard_map/ppermute | solution.py:53
  111.9 16.2 %collective-permute-start.18 = (bf16[128,2048]{1,0:T(8,128)(2,1)S(1)}, bf16[128,2048]{1,0:T(8,128)(2,1)S(1)}, u32[]{:S(2)}, u32[]{:S(2)}) collective-permute-start(bf16[128,2048]{1,0:T(8,128)(2,1)S(1)} %pad_maximum_fusion.1), channel_id=1, source_target_pairs={{0,6},{1,7},{2,0},{3,1},{4,2},{5,3},{6,4},{7,5},{8,14},{9,15},{10,... | collective-permute-start | bytes 1572872 | tf_op jit(solution)/shard_map/ppermute | solution.py:53
  115.7 16.5 %collective-permute-start.16 = (bf16[128,2048]{1,0:T(8,128)(2,1)S(1)}, bf16[128,2048]{1,0:T(8,128)(2,1)S(1)}, u32[]{:S(2)}, u32[]{:S(2)}) collective-permute-start(bf16[128,2048]{1,0:T(8,128)(2,1)S(1)} %pad_maximum_fusion), channel_id=1, source_target_pairs={{0,2},{1,3},{2,4},{3,5},{4,6},{5,7},{6,0},{7,1},{8,10},{9,11},{10,... | collective-permute-start | bytes 1572872 | tf_op jit(solution)/shard_map/ppermute | solution.py:53
  122.9 17.3 %collective-permute-start.12 = (bf16[64,2048]{1,0:T(8,128)(2,1)S(1)}, bf16[64,2048]{1,0:T(8,128)(2,1)S(1)}, u32[]{:S(2)}, u32[]{:S(2)}) collective-permute-start(bf16[64,2048]{1,0:T(8,128)(2,1)S(1)} %get-tuple-element.79), channel_id=1, source_target_pairs={{0,2},{1,3},{2,4},{3,5},{4,6},{5,7},{6,0},{7,1},{8,10},{9,11},{10,... | collective-permute-start | bytes 786440 | tf_op jit(solution)/shard_map/ppermute | solution.py:53
  124.3 15.9 %collective-permute-start.14 = (bf16[64,2048]{1,0:T(8,128)(2,1)S(1)}, bf16[64,2048]{1,0:T(8,128)(2,1)S(1)}, u32[]{:S(2)}, u32[]{:S(2)}) collective-permute-start(bf16[64,2048]{1,0:T(8,128)(2,1)S(1)} %get-tuple-element.80), channel_id=1, source_target_pairs={{0,6},{1,7},{2,0},{3,1},{4,2},{5,3},{6,4},{7,5},{8,14},{9,15},{10,... | collective-permute-start | bytes 786440 | tf_op jit(solution)/shard_map/ppermute | solution.py:53
  126.3 14.0 %collective-permute-start.13 = (bf16[64,2048]{1,0:T(8,128)(2,1)S(1)}, bf16[64,2048]{1,0:T(8,128)(2,1)S(1)}, u32[]{:S(2)}, u32[]{:S(2)}) collective-permute-start(bf16[64,2048]{1,0:T(8,128)(2,1)S(1)} %get-tuple-element.81), channel_id=1, source_target_pairs={{0,4},{1,5},{2,6},{3,7},{4,0},{5,1},{6,2},{7,3},{8,12},{9,13},{10,... | collective-permute-start | bytes 786440 | tf_op jit(solution)/shard_map/ppermute | solution.py:53
  132.4 8.1 %copy-start.3 = (bf16[1,64,4096]{2,1,0:T(8,128)(2,1)S(1)}, bf16[1,64,4096]{2,1,0:T(8,128)(2,1)}, u32[]{:S(2)}) copy-start(bf16[1,64,4096]{2,1,0:T(8,128)(2,1)} %param.16) | copy-start | bytes 1572868
  132.4 8.0 %collective-permute-start.19 = (bf16[64,2048]{1,0:T(8,128)(2,1)S(1)}, bf16[64,2048]{1,0:T(8,128)(2,1)S(1)}, u32[]{:S(2)}, u32[]{:S(2)}) collective-permute-start(bf16[64,2048]{1,0:T(8,128)(2,1)S(1)} %slice.72), channel_id=1, source_target_pairs={{0,8},{1,9},{2,10},{3,11},{4,12},{5,13},{6,14},{7,15},{8,0},{9,1},... | collective-permute-start | bytes 786440 | tf_op jit(solution)/shard_map/ppermute | solution.py:53
  (2 other events, 6.3 us)

commit v2 on v1

--- a/solution.py
+++ b/solution.py
@@ -42,7 +42,7 @@
 DOWN = feat_perm(lambda xl, z, c: (xl, (z + Z - 1) % Z, c))
 SWAP_X = feat_perm(lambda xl, z, c: (1 - xl, z, c))
 SWAP_C = feat_perm(lambda xl, z, c: (xl, z, 1 - c))
-OTHERS = ((0, 1), (0, 3), (1, 0), (0, 2), (1, 1), (1, 3), (1, 2))
+OTHERS = ((0, 1), (0, 3), (1, 2), (0, 2), (1, 0), (1, 1), (1, 3))
 
 
 def chip(dx, dz, xl, z, c):
@@ -57,23 +57,34 @@
     return lax.broadcasted_iota(I32, shape, dim)
 
 
-def index_kernel(where_ref, active_ref, slot_ref, rows_ref, cols_ref, meta_ref, most_ref, hits, rowt):
+def index_kernel(where_ref, active_ref, slot_ref, rows_ref, cols_ref, meta_ref, room_ref, hits, rowt):
     f = where_ref[0]
     xl, z, c = f // (Z * C), (f // C) % Z, f % C
-    for p in range(0, NPOS, 32):
-        slots = jnp.broadcast_to(slot_ref[p : p + 32, :], (32, 128))
-        for t in range(0, TOK, 128):
-            named = active_ref[:, t : t + 128]
-            hit = named[0:1, :] == slots
-            for k in range(1, active_ref.shape[0]):
-                hit = jnp.logical_or(hit, named[k : k + 1, :] == slots)
-            hits[p : p + 32, t : t + 128] = jnp.where(hit, 1.0, 0.0).astype(BF)
+    slots = []
+    for p in range(0, NPOS, 128):
+        row = jnp.broadcast_to(slot_ref[:, p : p + 128].astype(F32), (128, 128))
+        slots.append(jnp.transpose(row).astype(BF))
+    slots = jnp.concatenate(slots, axis=0)
+    one, zero = jnp.ones((16, 128), BF), jnp.zeros((16, 128), BF)
+    for t in range(0, TOK, 128):
+        named = active_ref[:, t : t + 128].astype(F32)
+        named = [
+            jnp.broadcast_to(named[k : k + 1, :], (16, 128)).astype(BF)
+            for k in range(named.shape[0])
+        ]
+        for p in range(0, NPOS, 16):
+            held = slots[p : p + 16, :]
+            hit = zero
+            for row in named:
+                hit = jnp.where(row == held, one, hit)
+            hits[p : p + 16, t : t + 128] = hit
     ones = jnp.ones((TOK, 128), BF)
     every = jnp.dot(hits[...], ones, preferred_element_type=F32)
     group = jnp.where(iota((OWN, NPOS), 1) // OWN == iota((OWN, NPOS), 0), 1.0, 0.0).astype(BF)
     units = jnp.floor((every + 15.0) * (1.0 / 16.0)).astype(BF)
     totals = jnp.dot(group, units, preferred_element_type=F32) * 16.0
-    most_ref[0, 0] = jnp.max(totals).astype(I32)
+    most = jnp.max(totals).astype(I32)
+    room_ref[0, 0] = sum((most > room).astype(I32) for room in ROOMS[:-1])
     other = f + 1 - 2 * c
     mine = jnp.concatenate(
         [hits[pl.ds(pl.multiple_of(o * OWN, OWN), OWN), :] for o in (f, other)], axis=0
@@ -336,7 +347,7 @@
     sections = lax.axis_size("section")
     where = jnp.stack([feat_index, section_index]).astype(I32)
     decoder = dec_weight[0]
-    rows, cols, meta, most = index_call(where, active.T, slot_block.reshape(NPOS, 1))
+    rows, cols, meta, room = index_call(where, active.T, slot_block.reshape(1, NPOS))
     near = [resid_in] + [move(resid_in, feat_perm(functools.partial(chip, *o))) for o in OTHERS]
     near = gather_call(where, near, meta)
     far = move(near, SWAP_C)
@@ -356,7 +367,7 @@
         return jnp.pad(act, ((0, FULL - room), (0, 0)))
 
     act = lax.switch(
-        sum((most[0, 0] > room).astype(I32) for room in ROOMS[:-1]),
+        room[0, 0],
         [functools.partial(exchange, room) for room in ROOMS],
         packed,
     )

time: 144 us -> 139 us (0.965); the launches traced: 142 us -> 139 us
  blocking collectives: 33.6 us -> 36.3 us
  waiting for transfers between devices: 29.7 us -> 27.2 us
  Pallas kernels: 43.1 us -> 41 us
    ppermute x20, waiting for transfers between devices: 29.7 us -> 27.2 us  [move(): return lax.ppermute(x, 'feat', pairs)]
    pallas_call x1, Pallas kernels: 4.86 us -> 2.7 us  [index_call(): pl.pallas_call(index_kernel, in_specs=[SM, VM, VM], out_specs=[VM, VM, VM...]
    all_to_all x1, blocking collectives: 19 us -> 20.5 us  [exchange(): parts = lax.all_to_all(parts, 'section', 0, 0)]
  transfers between devices with their start and end apart: 20 -> 20, of which waited for: 8 -> 10; matrix products, arithmetic and copies ran while one was open for 3% -> 3% of each run, Pallas kernels for 22% -> 21%
where the time goes in v2:
time: 139 us
  Pallas kernels  41 us (29%)
  blocking collectives  36.3 us (26%)
  starting transfers between devices  27.3 us (20%)
  waiting for transfers between devices  27.2 us (20%)
  matrix products  2.34 us (2%)
  local copies, waits for them, and re-layouts  2.09 us (2%)
  other arithmetic  2.01 us (1%)
    ppermute x20, starting transfers between devices, move(): return lax.ppermute(x, 'feat', pairs)  27.3 us
    ppermute x20, waiting for transfers between devices, move(): return lax.ppermute(x, 'feat', pairs)  27.2 us
    pallas_call x2, Pallas kernels, decode_call(): pl.pallas_call(functools.partial(decode_kernel, kind, half), grid=(steps,...  23.6 us
    all_to_all x1, blocking collectives, exchange(): parts = lax.all_to_all(parts, 'section', 0, 0)  20.5 us
    all_to_all x1, blocking collectives, exchange(): act = lax.all_to_all(wide, 'section', 0, 0).reshape(room, BLK)  15.7 us
    pallas_call x1, Pallas kernels, encode_call(): pl.pallas_call(encode_kernel, grid=(OWN // STEP,), in_specs=[SM, pl.Block...  7.58 us
    pallas_call x2, Pallas kernels, spread_call(): pl.pallas_call(functools.partial(spread_kernel, first), in_specs=[SM, VM,...  5.54 us
  transfers between devices with their start and end apart: 20, of which 10 were waited for; matrix products, arithmetic and copies ran while one was open for 3% of the time, Pallas kernels for 21%

profile of v2, /device:TPU:0, one launch (start us, length us, event | category | flops | bytes accessed | tf_op | source)
XLA Modules:
  0.0 139.3 jit_solution(13784852098741363625)
XLA Ops:
  0.0 2.9 %collective-permute-start.5 = (bf16[64,1024]{1,0:T(8,128)(2,1)}, bf16[64,1024]{1,0:T(8,128)(2,1)S(1)}, u32[]{:S(2)}, u32[]{:S(2)}) collective-permute-start(bf16[64,1024]{1,0:T(8,128)(2,1)} %refs_0_.1), channel_id=1, source_target_pairs={{0,10},{1,11},{2,12},{3,13},{4,14},{5,15},{6,8},{7,9},{8,2},{9,3},... | collective-permute-start | bytes 393224 | tf_op jit(solution)/shard_map/ppermute | solution.py:53
  3.5 3.6 %collective-permute-start.3 = (bf16[64,1024]{1,0:T(8,128)(2,1)}, bf16[64,1024]{1,0:T(8,128)(2,1)S(1)}, u32[]{:S(2)}, u32[]{:S(2)}) collective-permute-start(bf16[64,1024]{1,0:T(8,128)(2,1)} %refs_0_.1), channel_id=1, source_target_pairs={{0,4},{1,5},{2,6},{3,7},{4,0},{5,1},{6,2},{7,3},{8,12},{9,13},{10,... | collective-permute-start | bytes 393224 | tf_op jit(solution)/shard_map/ppermute | solution.py:53
  10.7 2.7 %collective-permute-start.6 = (bf16[64,1024]{1,0:T(8,128)(2,1)}, bf16[64,1024]{1,0:T(8,128)(2,1)S(1)}, u32[]{:S(2)}, u32[]{:S(2)}) collective-permute-start(bf16[64,1024]{1,0:T(8,128)(2,1)} %refs_0_.1), channel_id=1, source_target_pairs={{0,14},{1,15},{2,8},{3,9},{4,10},{5,11},{6,12},{7,13},{8,6},{9,7},... | collective-permute-start | bytes 393224 | tf_op jit(solution)/shard_map/ppermute | solution.py:53
  14.9 2.7 %shard_map.82 = (s32[32,1024]{1,0:T(8,128)S(1)}, s32[512,128]{1,0:T(8,128)S(1)}, s32[8,128]{1,0:T(8,128)S(1)}, s32[1,1]{1,0:T(1,128)}) custom-call(s32[2]{0:T(128)S(1)} %pad_add_fusion.where_ref, s32[24,1024]{1,0:T(8,128)S(1)} %bitcast.19, s32[1,256]{1,0:T(1,128)S(1)} %bitcast.20), custom_call_target="tpu_custom_call" | custom-call | flops 4294967296 | bytes 1048576 | tf_op jit(solution)/shard_map/pallas_call | solution.py:136
  19.1 2.6 %collective-permute-done.7.far_ref = bf16[512,1024]{1,0:T(8,128)(2,1)S(1)} collective-permute-done((bf16[512,1024]{1,0:T(8,128)(2,1)S(1)}, bf16[512,1024]{1,0:T(8,128)(2,1)S(1)}, u32[]{:S(2)}, u32[]{:S(2)}) %collective-permute-start.7) | collective-permute-done | bytes 1048608 | tf_op jit(solution)/shard_map/ppermute | solution.py:53
  22.5 2.3 %convolution_convert_fusion.half_ref = bf16[512,2048]{1,0:T(8,128)(2,1)S(1)} fusion(bf16[512,1024]{1,0:T(8,128)(2,1)S(1)} %shard_map.83, bf16[1024,2048]{1,0:T(8,128)(2,1)S(1)} %copy-done.1), kind=kOutput, calls=%fused_computation | convolution fusion | flops 2148532224 | bytes 7340032 | tf_op jit(solution)/shard_map/dot_general | solution.py:356
  24.9 7.6 %shard_map.84 = bf16[6144,128]{1,0:T(8,128)(2,1)S(1)} custom-call(s32[8,128]{1,0:T(8,128)S(1)} %get-tuple-element.62.refs_8_.meta_ref.after_ref, bf16[512,2048]{1,0:T(8,128)(2,1)S(1)} %convolution_convert_fusion.half_ref, bf16[512,1024]{1,0:T(8,128)(2,1)S(1)} %collective-permute-done.7.far_ref, s32[32,1024]{1,0:T(8,128)S(1)} %get-tuple-element.66.rows_ref, ...), custom_call_target="tpu_custom_call" | custom-call | flops 4294967296 | bytes 8388608 | tf_op jit(solution)/shard_map/pallas_call | solution.py:194
  32.5 37.7 %conditional.1 = (bf16[6144,128]{1,0:T(8,128)(2,1)S(1)}) conditional(s32[]{:T(128)} %bitcast.10, (bf16[6144,128]{1,0:T(8,128)(2,1)S(1)}, s32[2]{0:T(128)S(1)}, s32[8,128]{1,0:T(8,128)S(1)}, f32[16,128]{1,0:T(8,128)S(1)}) %tuple.24, (bf16[6144,128]{1,0:T(8,128)(2,1)S(1)}, s32[2]{0:T(128)S(1)}, s32[8,128]{1,0:T(8,128)S(1)}, ...), branch_computations={%region_0.1_spmd, %region_1.2_spmd, %region_2.3_spmd} | conditional | flops 16777216 | bytes 12255240 | solution.py:369
  32.5 20.5 %all_to_all.24.parts_ref = bf16[8,320,128]{2,1,0:T(8,128)(2,1)S(1)} all-to-all(bf16[8,320,128]{2,1,0:T(8,128)(2,1)S(1)} %bitcast.28), channel_id=1, replica_groups=mesh['section'=8,'feat'=16] {'section'}, dimensions={0} | all-to-all | bytes 1310720 | tf_op jit(solution)/shard_map/cond/branch_0_fun/all_to_all | solution.py:363
  54.1 15.7 %all_to_all.25 = bf16[8,320,128]{2,1,0:T(8,128)(2,1)S(1)} all-to-all(bf16[8,320,128]{2,1,0:T(8,128)(2,1)S(1)} %broadcast_in_dim.11), channel_id=1, replica_groups=mesh['section'=8,'feat'=16] {'section'}, dimensions={0} | all-to-all | bytes 1310720 | tf_op jit(solution)/shard_map/cond/branch_0_fun/all_to_all | solution.py:366
  70.3 2.6 %shard_map.85.a1_ref = bf16[512,2048]{1,0:T(8,128)(2,1)S(1)} custom-call(s32[8,128]{1,0:T(8,128)S(1)} %get-tuple-element.62.refs_8_.meta_ref.after_ref, s32[512,128]{1,0:T(8,128)S(1)} %get-tuple-element.63.cols_ref, bf16[6144,128]{1,0:T(8,128)(2,1)S(1)} %get-tuple-element.82.act_ref), custom_call_target="tpu_custom_call" | custom-call | flops 1073741824 | bytes 4194304 | tf_op jit(solution)/shard_map/pallas_call | solution.py:263
  73.7 2.9 %shard_map.86.a2_ref = bf16[512,2048]{1,0:T(8,128)(2,1)S(1)} custom-call(s32[8,128]{1,0:T(8,128)S(1)} %get-tuple-element.62.refs_8_.meta_ref.after_ref, s32[512,128]{1,0:T(8,128)S(1)} %get-tuple-element.63.cols_ref, bf16[6144,128]{1,0:T(8,128)(2,1)S(1)} %collective-permute-done.8.act_ref), custom_call_target="tpu_custom_call" | custom-call | flops 1073741824 | bytes 4194304 | tf_op jit(solution)/shard_map/pallas_call | solution.py:263
  76.6 11.7 %shard_map.87 = (bf16[256,2048]{1,0:T(8,128)(2,1)S(1)}, bf16[256,2048]{1,0:T(8,128)(2,1)S(1)}) custom-call(bf16[512,2048]{1,0:T(8,128)(2,1)S(1)} %shard_map.85.a1_ref, bf16[512,2048]{1,0:T(8,128)(2,1)S(1)} %shard_map.86.a2_ref, bf16[2048,4096]{1,0:T(8,128)(2,1)} %bitcast.22, bf16[2048,4096]{1,0:T(8,128)(2,1)} %collective-permute-done.9.w2_ref, ...), custom_call_target="tpu_custom_call" | custom-call | flops 8589934592 | bytes 23068672 | tf_op jit(solution)/shard_map/pallas_call | solution.py:309
  89.5 12.0 %shard_map.88 = (bf16[128,2048]{1,0:T(8,128)(2,1)S(1)}, bf16[128,2048]{1,0:T(8,128)(2,1)S(1)}, bf16[128,2048]{1,0:T(8,128)(2,1)S(1)}, bf16[128,1024]{1,0:T(8,128)(2,1)S(1)}, bf16[128,1024]{1,0:T(8,128)(2,1)S(1)}) custom-call(bf16[512,2048]{1,0:T(8,128)(2,1)S(1)} %shard_map.85.a1_ref, bf16[512,2048]{1,0:T(8,128)(2,1)S(1)} %shard_map.86.a2_ref, ...), custom_call_target="tpu_custom_call" | custom-call | flops 8589934592 | bytes 23068672 | tf_op jit(solution)/shard_map/pallas_call | solution.py:309
  102.3 1.5 %collective-permute-start.15 = (bf16[128,1024]{1,0:T(8,128)(2,1)S(1)}, bf16[128,1024]{1,0:T(8,128)(2,1)S(1)}, u32[]{:S(2)}, u32[]{:S(2)}) collective-permute-start(bf16[128,1024]{1,0:T(8,128)(2,1)S(1)} %get-tuple-element.76), channel_id=1, source_target_pairs={{0,2},{1,3},{2,4},{3,5},{4,6},{5,7},{6,0},{7,1},{8,10},{9,11},{10,... | collective-permute-start | bytes 786440 | tf_op jit(solution)/shard_map/ppermute | solution.py:53
  104.9 4.7 %collective-permute-done.17 = bf16[128,1024]{1,0:T(8,128)(2,1)S(1)} collective-permute-done((bf16[128,1024]{1,0:T(8,128)(2,1)S(1)}, bf16[128,1024]{1,0:T(8,128)(2,1)S(1)}, u32[]{:S(2)}, u32[]{:S(2)}) %collective-permute-start.17) | collective-permute-done | bytes 262176 | tf_op jit(solution)/shard_map/ppermute | solution.py:53
  109.7 2.5 %collective-permute-start.18 = (bf16[128,2048]{1,0:T(8,128)(2,1)S(1)}, bf16[128,2048]{1,0:T(8,128)(2,1)S(1)}, u32[]{:S(2)}, u32[]{:S(2)}) collective-permute-start(bf16[128,2048]{1,0:T(8,128)(2,1)S(1)} %pad_maximum_fusion.1), channel_id=1, source_target_pairs={{0,6},{1,7},{2,0},{3,1},{4,2},{5,3},{6,4},{7,5},{8,14},{9,15},{10,... | collective-permute-start | bytes 1572872 | tf_op jit(solution)/shard_map/ppermute | solution.py:53
  112.5 7.2 %collective-permute-done.11 = bf16[256,1280]{1,0:T(8,128)(2,1)S(1)} collective-permute-done((bf16[256,1280]{1,0:T(8,128)(2,1)S(1)}, bf16[256,1280]{1,0:T(8,128)(2,1)S(1)}, u32[]{:S(2)}, u32[]{:S(2)}) %collective-permute-start.11) | collective-permute-done | bytes 655392 | tf_op jit(solution)/shard_map/ppermute | solution.py:53
  120.0 1.9 %collective-permute-start.12 = (bf16[64,2048]{1,0:T(8,128)(2,1)S(1)}, bf16[64,2048]{1,0:T(8,128)(2,1)S(1)}, u32[]{:S(2)}, u32[]{:S(2)}) collective-permute-start(bf16[64,2048]{1,0:T(8,128)(2,1)S(1)} %get-tuple-element.79), channel_id=1, source_target_pairs={{0,2},{1,3},{2,4},{3,5},{4,6},{5,7},{6,0},{7,1},{8,10},{9,11},{10,... | collective-permute-start | bytes 786440 | tf_op jit(solution)/shard_map/ppermute | solution.py:53
  122.0 1.4 collective-permute-start.14
  123.3 2.4 %collective-permute-start.13 = (bf16[64,2048]{1,0:T(8,128)(2,1)S(1)}, bf16[64,2048]{1,0:T(8,128)(2,1)S(1)}, u32[]{:S(2)}, u32[]{:S(2)}) collective-permute-start(bf16[64,2048]{1,0:T(8,128)(2,1)S(1)} %get-tuple-element.81), channel_id=1, source_target_pairs={{0,4},{1,5},{2,6},{3,7},{4,0},{5,1},{6,2},{7,3},{8,12},{9,13},{10,... | collective-permute-start | bytes 786440 | tf_op jit(solution)/shard_map/ppermute | solution.py:53
  125.7 2.8 %collective-permute-done.16 = bf16[128,2048]{1,0:T(8,128)(2,1)S(1)} collective-permute-done((bf16[128,2048]{1,0:T(8,128)(2,1)S(1)}, bf16[128,2048]{1,0:T(8,128)(2,1)S(1)}, u32[]{:S(2)}, u32[]{:S(2)}) %collective-permute-start.16) | collective-permute-done | bytes 524320 | tf_op jit(solution)/shard_map/ppermute | solution.py:53
  128.8 1.8 %collective-permute-start.19 = (bf16[64,2048]{1,0:T(8,128)(2,1)S(1)}, bf16[64,2048]{1,0:T(8,128)(2,1)S(1)}, u32[]{:S(2)}, u32[]{:S(2)}) collective-permute-start(bf16[64,2048]{1,0:T(8,128)(2,1)S(1)} %slice.72), channel_id=1, source_target_pairs={{0,8},{1,9},{2,10},{3,11},{4,12},{5,13},{6,14},{7,15},{8,0},{9,1},... | collective-permute-start | bytes 786440 | tf_op jit(solution)/shard_map/ppermute | solution.py:53
  130.5 7.5 %collective-permute-done.12 = bf16[64,2048]{1,0:T(8,128)(2,1)S(1)} collective-permute-done((bf16[64,2048]{1,0:T(8,128)(2,1)S(1)}, bf16[64,2048]{1,0:T(8,128)(2,1)S(1)}, u32[]{:S(2)}, u32[]{:S(2)}) %collective-permute-start.12) | collective-permute-done | bytes 262176 | tf_op jit(solution)/shard_map/ppermute | solution.py:53
  (62 shorter events, 14.6 us)
Async XLA Ops:
  0.0 9.6 %collective-permute-start.5 = (bf16[64,1024]{1,0:T(8,128)(2,1)}, bf16[64,1024]{1,0:T(8,128)(2,1)S(1)}, u32[]{:S(2)}, u32[]{:S(2)}) collective-permute-start(bf16[64,1024]{1,0:T(8,128)(2,1)} %refs_0_.1), channel_id=1, source_target_pairs={{0,10},{1,11},{2,12},{3,13},{4,14},{5,15},{6,8},{7,9},{8,2},{9,3},... | collective-permute-start | bytes 393224 | tf_op jit(solution)/shard_map/ppermute | solution.py:53
  2.9 7.8 %collective-permute-start.4 = (bf16[64,1024]{1,0:T(8,128)(2,1)}, bf16[64,1024]{1,0:T(8,128)(2,1)S(1)}, u32[]{:S(2)}, u32[]{:S(2)}) collective-permute-start(bf16[64,1024]{1,0:T(8,128)(2,1)} %refs_0_.1), channel_id=1, source_target_pairs={{0,8},{1,9},{2,10},{3,11},{4,12},{5,13},{6,14},{7,15},{8,0},{9,1},... | collective-permute-start | bytes 393224 | tf_op jit(solution)/shard_map/ppermute | solution.py:53
  3.5 14.2 %collective-permute-start.3 = (bf16[64,1024]{1,0:T(8,128)(2,1)}, bf16[64,1024]{1,0:T(8,128)(2,1)S(1)}, u32[]{:S(2)}, u32[]{:S(2)}) collective-permute-start(bf16[64,1024]{1,0:T(8,128)(2,1)} %refs_0_.1), channel_id=1, source_target_pairs={{0,4},{1,5},{2,6},{3,7},{4,0},{5,1},{6,2},{7,3},{8,12},{9,13},{10,... | collective-permute-start | bytes 393224 | tf_op jit(solution)/shard_map/ppermute | solution.py:53
  7.0 10.6 %collective-permute-start.2 = (bf16[64,1024]{1,0:T(8,128)(2,1)}, bf16[64,1024]{1,0:T(8,128)(2,1)S(1)}, u32[]{:S(2)}, u32[]{:S(2)}) collective-permute-start(bf16[64,1024]{1,0:T(8,128)(2,1)} %refs_0_.1), channel_id=1, source_target_pairs={{0,12},{1,13},{2,14},{3,15},{4,8},{5,9},{6,10},{7,11},{8,4},{9,5},... | collective-permute-start | bytes 393224 | tf_op jit(solution)/shard_map/ppermute | solution.py:53
  8.0 10.2 %collective-permute-start.1 = (bf16[64,1024]{1,0:T(8,128)(2,1)}, bf16[64,1024]{1,0:T(8,128)(2,1)S(1)}, u32[]{:S(2)}, u32[]{:S(2)}) collective-permute-start(bf16[64,1024]{1,0:T(8,128)(2,1)} %refs_0_.1), channel_id=1, source_target_pairs={{0,6},{1,7},{2,0},{3,1},{4,2},{5,3},{6,4},{7,5},{8,14},{9,15},{10,... | collective-permute-start | bytes 393224 | tf_op jit(solution)/shard_map/ppermute | solution.py:53
  9.6 8.7 %collective-permute-start = (bf16[64,1024]{1,0:T(8,128)(2,1)}, bf16[64,1024]{1,0:T(8,128)(2,1)S(1)}, u32[]{:S(2)}, u32[]{:S(2)}) collective-permute-start(bf16[64,1024]{1,0:T(8,128)(2,1)} %refs_0_.1), channel_id=1, source_target_pairs={{0,2},{1,3},{2,4},{3,5},{4,6},{5,7},{6,0},{7,1},{8,10},{9,11},{10,... | collective-permute-start | bytes 393224 | tf_op jit(solution)/shard_map/ppermute | solution.py:53
  10.7 7.6 %collective-permute-start.6 = (bf16[64,1024]{1,0:T(8,128)(2,1)}, bf16[64,1024]{1,0:T(8,128)(2,1)S(1)}, u32[]{:S(2)}, u32[]{:S(2)}) collective-permute-start(bf16[64,1024]{1,0:T(8,128)(2,1)} %refs_0_.1), channel_id=1, source_target_pairs={{0,14},{1,15},{2,8},{3,9},{4,10},{5,11},{6,12},{7,13},{8,6},{9,7},... | collective-permute-start | bytes 393224 | tf_op jit(solution)/shard_map/ppermute | solution.py:53
  14.9 7.6 %copy-start.1 = (bf16[1024,2048]{1,0:T(8,128)(2,1)S(1)}, bf16[1024,2048]{1,0:T(8,128)(2,1)}, u32[]{:S(2)}) copy-start(bf16[1024,2048]{1,0:T(8,128)(2,1)} %enc_ref.1) | copy-start | bytes 12582916
  19.0 2.7 %collective-permute-start.7 = (bf16[512,1024]{1,0:T(8,128)(2,1)S(1)}, bf16[512,1024]{1,0:T(8,128)(2,1)S(1)}, u32[]{:S(2)}, u32[]{:S(2)}) collective-permute-start(bf16[512,1024]{1,0:T(8,128)(2,1)S(1)} %shard_map.83), channel_id=1, source_target_pairs={{0,1},{1,0},{2,3},{3,2},{4,5},{5,4},{6,7},{7,6},{8,9},{9,8},{10,11... | collective-permute-start | bytes 3145736 | tf_op jit(solution)/shard_map/ppermute | solution.py:53
  21.7 54.8 %collective-permute-start.9 = (bf16[2048,4096]{1,0:T(8,128)(2,1)}, bf16[2048,4096]{1,0:T(8,128)(2,1)}, u32[]{:S(2)}, u32[]{:S(2)}) collective-permute-start(bf16[2048,4096]{1,0:T(8,128)(2,1)} %bitcast.21), channel_id=1, source_target_pairs={{0,1},{1,0},{2,3},{3,2},{4,5},{5,4},{6,7},{7,6},{8,9},{9,8},{10,11... | collective-permute-start | bytes 50331656 | tf_op jit(solution)/shard_map/ppermute | solution.py:53
  24.9 7.6 %copy-start.5 = (f32[2048]{0:T(1024)S(1)}, f32[2048]{0:T(1024)}, u32[]{:S(2)}) copy-start(f32[2048]{0:T(1024)} %param.14) | copy-start | bytes 24580
  70.2 3.5 %collective-permute-start.8 = (bf16[6144,128]{1,0:T(8,128)(2,1)S(1)}, bf16[6144,128]{1,0:T(8,128)(2,1)S(1)}, u32[]{:S(2)}, u32[]{:S(2)}) collective-permute-start(bf16[6144,128]{1,0:T(8,128)(2,1)S(1)} %get-tuple-element.82.act_ref), channel_id=1, source_target_pairs={{0,1},{1,0},{2,3},{3,2},{4,5},{5,4},{6,7},{7,6},{8,9},{9,8},{10,11... | collective-permute-start | bytes 4718600 | tf_op jit(solution)/shard_map/ppermute | solution.py:53
  88.3 13.2 %collective-permute-start.10 = (bf16[256,768]{1,0:T(8,128)(2,1)S(1)}, bf16[256,768]{1,0:T(8,128)(2,1)S(1)}, u32[]{:S(2)}, u32[]{:S(2)}) collective-permute-start(bf16[256,768]{1,0:T(8,128)(2,1)S(1)} %slice.48), channel_id=1, source_target_pairs={{0,8},{1,9},{2,10},{3,11},{4,12},{5,13},{6,14},{7,15},{8,0},{9,1},... | collective-permute-start | bytes 1179656 | tf_op jit(solution)/shard_map/ppermute | solution.py:53
  89.5 12.7 %copy-start.6 = (s32[64]{0:T(128)S(1)}, s32[64]{0:T(128)}, u32[]{:S(2)}) copy-start(s32[64]{0:T(128)} %param.18) | copy-start | bytes 772
  101.6 8.0 %collective-permute-start.17 = (bf16[128,1024]{1,0:T(8,128)(2,1)S(1)}, bf16[128,1024]{1,0:T(8,128)(2,1)S(1)}, u32[]{:S(2)}, u32[]{:S(2)}) collective-permute-start(bf16[128,1024]{1,0:T(8,128)(2,1)S(1)} %get-tuple-element.78), channel_id=1, source_target_pairs={{0,6},{1,7},{2,0},{3,1},{4,2},{5,3},{6,4},{7,5},{8,14},{9,15},{10,... | collective-permute-start | bytes 786440 | tf_op jit(solution)/shard_map/ppermute | solution.py:53
  102.3 10.0 %collective-permute-start.15 = (bf16[128,1024]{1,0:T(8,128)(2,1)S(1)}, bf16[128,1024]{1,0:T(8,128)(2,1)S(1)}, u32[]{:S(2)}, u32[]{:S(2)}) collective-permute-start(bf16[128,1024]{1,0:T(8,128)(2,1)S(1)} %get-tuple-element.76), channel_id=1, source_target_pairs={{0,2},{1,3},{2,4},{3,5},{4,6},{5,7},{6,0},{7,1},{8,10},{9,11},{10,... | collective-permute-start | bytes 786440 | tf_op jit(solution)/shard_map/ppermute | solution.py:53
  103.8 15.9 %collective-permute-start.11 = (bf16[256,1280]{1,0:T(8,128)(2,1)S(1)}, bf16[256,1280]{1,0:T(8,128)(2,1)S(1)}, u32[]{:S(2)}, u32[]{:S(2)}) collective-permute-start(bf16[256,1280]{1,0:T(8,128)(2,1)S(1)} %slice.47), channel_id=1, source_target_pairs={{0,8},{1,9},{2,10},{3,11},{4,12},{5,13},{6,14},{7,15},{8,0},{9,1},... | collective-permute-start | bytes 1966088 | tf_op jit(solution)/shard_map/ppermute | solution.py:53
  109.7 16.0 %collective-permute-start.18 = (bf16[128,2048]{1,0:T(8,128)(2,1)S(1)}, bf16[128,2048]{1,0:T(8,128)(2,1)S(1)}, u32[]{:S(2)}, u32[]{:S(2)}) collective-permute-start(bf16[128,2048]{1,0:T(8,128)(2,1)S(1)} %pad_maximum_fusion.1), channel_id=1, source_target_pairs={{0,6},{1,7},{2,0},{3,1},{4,2},{5,3},{6,4},{7,5},{8,14},{9,15},{10,... | collective-permute-start | bytes 1572872 | tf_op jit(solution)/shard_map/ppermute | solution.py:53
  112.4 16.1 %collective-permute-start.16 = (bf16[128,2048]{1,0:T(8,128)(2,1)S(1)}, bf16[128,2048]{1,0:T(8,128)(2,1)S(1)}, u32[]{:S(2)}, u32[]{:S(2)}) collective-permute-start(bf16[128,2048]{1,0:T(8,128)(2,1)S(1)} %pad_maximum_fusion), channel_id=1, source_target_pairs={{0,2},{1,3},{2,4},{3,5},{4,6},{5,7},{6,0},{7,1},{8,10},{9,11},{10,... | collective-permute-start | bytes 1572872 | tf_op jit(solution)/shard_map/ppermute | solution.py:53
  120.0 18.1 %collective-permute-start.12 = (bf16[64,2048]{1,0:T(8,128)(2,1)S(1)}, bf16[64,2048]{1,0:T(8,128)(2,1)S(1)}, u32[]{:S(2)}, u32[]{:S(2)}) collective-permute-start(bf16[64,2048]{1,0:T(8,128)(2,1)S(1)} %get-tuple-element.79), channel_id=1, source_target_pairs={{0,2},{1,3},{2,4},{3,5},{4,6},{5,7},{6,0},{7,1},{8,10},{9,11},{10,... | collective-permute-start | bytes 786440 | tf_op jit(solution)/shard_map/ppermute | solution.py:53
  122.0 16.1 %collective-permute-start.14 = (bf16[64,2048]{1,0:T(8,128)(2,1)S(1)}, bf16[64,2048]{1,0:T(8,128)(2,1)S(1)}, u32[]{:S(2)}, u32[]{:S(2)}) collective-permute-start(bf16[64,2048]{1,0:T(8,128)(2,1)S(1)} %get-tuple-element.80), channel_id=1, source_target_pairs={{0,6},{1,7},{2,0},{3,1},{4,2},{5,3},{6,4},{7,5},{8,14},{9,15},{10,... | collective-permute-start | bytes 786440 | tf_op jit(solution)/shard_map/ppermute | solution.py:53
  123.3 14.8 %collective-permute-start.13 = (bf16[64,2048]{1,0:T(8,128)(2,1)S(1)}, bf16[64,2048]{1,0:T(8,128)(2,1)S(1)}, u32[]{:S(2)}, u32[]{:S(2)}) collective-permute-start(bf16[64,2048]{1,0:T(8,128)(2,1)S(1)} %get-tuple-element.81), channel_id=1, source_target_pairs={{0,4},{1,5},{2,6},{3,7},{4,0},{5,1},{6,2},{7,3},{8,12},{9,13},{10,... | collective-permute-start | bytes 786440 | tf_op jit(solution)/shard_map/ppermute | solution.py:53
  128.7 9.6 %copy-start.4 = (bf16[1,64,4096]{2,1,0:T(8,128)(2,1)S(1)}, bf16[1,64,4096]{2,1,0:T(8,128)(2,1)}, u32[]{:S(2)}) copy-start(bf16[1,64,4096]{2,1,0:T(8,128)(2,1)} %param.16) | copy-start | bytes 1572868
  128.8 9.4 %collective-permute-start.19 = (bf16[64,2048]{1,0:T(8,128)(2,1)S(1)}, bf16[64,2048]{1,0:T(8,128)(2,1)S(1)}, u32[]{:S(2)}, u32[]{:S(2)}) collective-permute-start(bf16[64,2048]{1,0:T(8,128)(2,1)S(1)} %slice.72), channel_id=1, source_target_pairs={{0,8},{1,9},{2,10},{3,11},{4,12},{5,13},{6,14},{7,15},{8,0},{9,1},... | collective-permute-start | bytes 786440 | tf_op jit(solution)/shard_map/ppermute | solution.py:53
  (3 other events, 5.0 us)

commit v3 on v2

--- a/solution.py
+++ b/solution.py
@@ -14,7 +14,7 @@
 NPOS = 256
 OWN = 16
 FULL = OWN * CAP
-ROOMS = (2560, 3072, FULL)
+ROOMS = (2560, 2816, 3072, FULL)
 WIN = 128
 STEP = 8
 EARLY = 768
@@ -351,9 +351,9 @@
     near = [resid_in] + [move(resid_in, feat_perm(functools.partial(chip, *o))) for o in OTHERS]
     near = gather_call(where, near, meta)
     far = move(near, SWAP_C)
-    leaving, far = lax.optimization_barrier((decoder, far))
+    half = jnp.dot(near, enc_weight, preferred_element_type=F32).astype(BF)
+    leaving, half, far = lax.optimization_barrier((decoder, half, far))
     other_decoder = move(leaving, SWAP_C)
-    half = jnp.dot(near, enc_weight, preferred_element_type=F32).astype(BF)
     packed = encode_call(meta, half, far, rows, enc_weight)
     bias = enc_bias.reshape(OWN, BLK)
 

time: 139 us -> 137 us (0.986)
  waiting for transfers between devices: 27.2 us -> 24 us
  blocking collectives: 36.3 us -> 34.6 us
  Pallas kernels: 41 us -> 42.4 us
    ppermute x20, waiting for transfers between devices: 27.2 us -> 24 us  [move(): return lax.ppermute(x, 'feat', pairs)]
  transfers between devices with their start and end apart: 20 -> 20, of which waited for: 10 -> 10; matrix products, arithmetic and copies ran while one was open for 3% -> 3% of each run, Pallas kernels for 21% -> 22%
where the time goes in v3:
time: 137 us
  Pallas kernels  42.4 us (31%)
  blocking collectives  34.6 us (25%)
  starting transfers between devices  28 us (20%)
  waiting for transfers between devices  24 us (18%)
  matrix products  2.34 us (2%)
  local copies, waits for them, and re-layouts  2.09 us (2%)
  other arithmetic  2.01 us (1%)
    ppermute x20, starting transfers between devices, move(): return lax.ppermute(x, 'feat', pairs)  28 us
    ppermute x20, waiting for transfers between devices, move(): return lax.ppermute(x, 'feat', pairs)  24 us
    pallas_call x2, Pallas kernels, decode_call(): pl.pallas_call(functools.partial(decode_kernel, kind, half), grid=(steps,...  23.7 us
    all_to_all x1, blocking collectives, exchange(): parts = lax.all_to_all(parts, 'section', 0, 0)  19.8 us
    all_to_all x1, blocking collectives, exchange(): act = lax.all_to_all(wide, 'section', 0, 0).reshape(room, BLK)  14.8 us
    pallas_call x1, Pallas kernels, encode_call(): pl.pallas_call(encode_kernel, grid=(OWN // STEP,), in_specs=[SM, pl.Block...  8.17 us
    pallas_call x2, Pallas kernels, spread_call(): pl.pallas_call(functools.partial(spread_kernel, first), in_specs=[SM, VM,...  6.33 us
  transfers between devices with their start and end apart: 20, of which 10 were waited for; matrix products, arithmetic and copies ran while one was open for 3% of the time, Pallas kernels for 22%

profile of v3, /device:TPU:0, one launch (start us, length us, event | category | flops | bytes accessed | tf_op | source)
XLA Modules:
  0.0 136.6 jit_solution(15422066116527844713)
XLA Ops:
  0.0 2.9 %collective-permute-start.5 = (bf16[64,1024]{1,0:T(8,128)(2,1)}, bf16[64,1024]{1,0:T(8,128)(2,1)S(1)}, u32[]{:S(2)}, u32[]{:S(2)}) collective-permute-start(bf16[64,1024]{1,0:T(8,128)(2,1)} %refs_0_.1), channel_id=1, source_target_pairs={{0,10},{1,11},{2,12},{3,13},{4,14},{5,15},{6,8},{7,9},{8,2},{9,3},... | collective-permute-start | bytes 393224 | tf_op jit(solution)/shard_map/ppermute | solution.py:53
  3.5 3.6 %collective-permute-start.3 = (bf16[64,1024]{1,0:T(8,128)(2,1)}, bf16[64,1024]{1,0:T(8,128)(2,1)S(1)}, u32[]{:S(2)}, u32[]{:S(2)}) collective-permute-start(bf16[64,1024]{1,0:T(8,128)(2,1)} %refs_0_.1), channel_id=1, source_target_pairs={{0,4},{1,5},{2,6},{3,7},{4,0},{5,1},{6,2},{7,3},{8,12},{9,13},{10,... | collective-permute-start | bytes 393224 | tf_op jit(solution)/shard_map/ppermute | solution.py:53
  8.0 1.3 collective-permute-start.1
  10.7 2.7 %collective-permute-start.6 = (bf16[64,1024]{1,0:T(8,128)(2,1)}, bf16[64,1024]{1,0:T(8,128)(2,1)S(1)}, u32[]{:S(2)}, u32[]{:S(2)}) collective-permute-start(bf16[64,1024]{1,0:T(8,128)(2,1)} %refs_0_.1), channel_id=1, source_target_pairs={{0,14},{1,15},{2,8},{3,9},{4,10},{5,11},{6,12},{7,13},{8,6},{9,7},... | collective-permute-start | bytes 393224 | tf_op jit(solution)/shard_map/ppermute | solution.py:53
  14.9 2.7 %shard_map.82 = (s32[32,1024]{1,0:T(8,128)S(1)}, s32[512,128]{1,0:T(8,128)S(1)}, s32[8,128]{1,0:T(8,128)S(1)}, s32[1,1]{1,0:T(1,128)}) custom-call(s32[2]{0:T(128)S(1)} %pad_add_fusion.where_ref, s32[24,1024]{1,0:T(8,128)S(1)} %bitcast.21, s32[1,256]{1,0:T(1,128)S(1)} %bitcast.22), custom_call_target="tpu_custom_call" | custom-call | flops 4294967296 | bytes 1048576 | tf_op jit(solution)/shard_map/pallas_call | solution.py:136
  19.1 2.3 %convolution_convert_fusion.half_ref = bf16[512,2048]{1,0:T(8,128)(2,1)S(1)} fusion(bf16[512,1024]{1,0:T(8,128)(2,1)S(1)} %shard_map.83, bf16[1024,2048]{1,0:T(8,128)(2,1)S(1)} %copy-done.1), kind=kOutput, calls=%fused_computation | convolution fusion | flops 2148532224 | bytes 7340032 | tf_op jit(solution)/shard_map/dot_general | solution.py:354
  22.7 8.2 %shard_map.84 = bf16[6144,128]{1,0:T(8,128)(2,1)S(1)} custom-call(s32[8,128]{1,0:T(8,128)S(1)} %get-tuple-element.76.refs_8_.meta_ref.after_ref, bf16[512,2048]{1,0:T(8,128)(2,1)S(1)} %convolution_convert_fusion.half_ref, bf16[512,1024]{1,0:T(8,128)(2,1)S(1)} %collective-permute-done.7.far_ref, s32[32,1024]{1,0:T(8,128)S(1)} %get-tuple-element.81.rows_ref, ...), custom_call_target="tpu_custom_call" | custom-call | flops 4294967296 | bytes 8388608 | tf_op jit(solution)/shard_map/pallas_call | solution.py:194
  30.9 36.0 %conditional.1 = (bf16[6144,128]{1,0:T(8,128)(2,1)S(1)}) conditional(s32[]{:T(128)} %bitcast.12, (bf16[6144,128]{1,0:T(8,128)(2,1)S(1)}, s32[2]{0:T(128)S(1)}, s32[8,128]{1,0:T(8,128)S(1)}, f32[16,128]{1,0:T(8,128)S(1)}) %tuple.28, (bf16[6144,128]{1,0:T(8,128)(2,1)S(1)}, s32[2]{0:T(128)S(1)}, s32[8,128]{1,0:T(8,128)S(1)}, ...), branch_computations={%region_0.1_spmd, %region_1.2_spmd, %region_2.3_spmd, %region_3.4_... | conditional | flops 16777216 | bytes 12255240 | solution.py:369
  31.0 19.8 %all_to_all.32.parts_ref = bf16[8,320,128]{2,1,0:T(8,128)(2,1)S(1)} all-to-all(bf16[8,320,128]{2,1,0:T(8,128)(2,1)S(1)} %bitcast.29), channel_id=1, replica_groups=mesh['section'=8,'feat'=16] {'section'}, dimensions={0} | all-to-all | bytes 1310720 | tf_op jit(solution)/shard_map/cond/branch_0_fun/all_to_all | solution.py:363
  51.8 14.8 %all_to_all.33 = bf16[8,320,128]{2,1,0:T(8,128)(2,1)S(1)} all-to-all(bf16[8,320,128]{2,1,0:T(8,128)(2,1)S(1)} %broadcast_in_dim.16), channel_id=1, replica_groups=mesh['section'=8,'feat'=16] {'section'}, dimensions={0} | all-to-all | bytes 1310720 | tf_op jit(solution)/shard_map/cond/branch_0_fun/all_to_all | solution.py:366
  67.0 3.2 %shard_map.85.a1_ref = bf16[512,2048]{1,0:T(8,128)(2,1)S(1)} custom-call(s32[8,128]{1,0:T(8,128)S(1)} %get-tuple-element.76.refs_8_.meta_ref.after_ref, s32[512,128]{1,0:T(8,128)S(1)} %get-tuple-element.77.cols_ref, bf16[6144,128]{1,0:T(8,128)(2,1)S(1)} %get-tuple-element.97.act_ref), custom_call_target="tpu_custom_call" | custom-call | flops 1073741824 | bytes 4194304 | tf_op jit(solution)/shard_map/pallas_call | solution.py:263
  70.4 3.1 %shard_map.86.a2_ref = bf16[512,2048]{1,0:T(8,128)(2,1)S(1)} custom-call(s32[8,128]{1,0:T(8,128)S(1)} %get-tuple-element.76.refs_8_.meta_ref.after_ref, s32[512,128]{1,0:T(8,128)S(1)} %get-tuple-element.77.cols_ref, bf16[6144,128]{1,0:T(8,128)(2,1)S(1)} %collective-permute-done.8.act_ref), custom_call_target="tpu_custom_call" | custom-call | flops 1073741824 | bytes 4194304 | tf_op jit(solution)/shard_map/pallas_call | solution.py:263
  73.6 11.7 %shard_map.87 = (bf16[256,2048]{1,0:T(8,128)(2,1)S(1)}, bf16[256,2048]{1,0:T(8,128)(2,1)S(1)}) custom-call(bf16[512,2048]{1,0:T(8,128)(2,1)S(1)} %shard_map.85.a1_ref, bf16[512,2048]{1,0:T(8,128)(2,1)S(1)} %shard_map.86.a2_ref, bf16[2048,4096]{1,0:T(8,128)(2,1)} %bitcast.13.w1_ref, bf16[2048,4096]{1,0:T(8,128)(2,1)} %collective-permute-done.9.w2_ref, ...), custom_call_target="tpu_custom_call" | custom-call | flops 8589934592 | bytes 23068672 | tf_op jit(solution)/shard_map/pallas_call | solution.py:309
  85.9 12.0 %shard_map.88 = (bf16[128,2048]{1,0:T(8,128)(2,1)S(1)}, bf16[128,2048]{1,0:T(8,128)(2,1)S(1)}, bf16[128,2048]{1,0:T(8,128)(2,1)S(1)}, bf16[128,1024]{1,0:T(8,128)(2,1)S(1)}, bf16[128,1024]{1,0:T(8,128)(2,1)S(1)}) custom-call(bf16[512,2048]{1,0:T(8,128)(2,1)S(1)} %shard_map.85.a1_ref, bf16[512,2048]{1,0:T(8,128)(2,1)S(1)} %shard_map.86.a2_ref, ...), custom_call_target="tpu_custom_call" | custom-call | flops 8589934592 | bytes 23068672 | tf_op jit(solution)/shard_map/pallas_call | solution.py:309
  97.9 2.8 %collective-permute-start.17 = (bf16[128,1024]{1,0:T(8,128)(2,1)S(1)}, bf16[128,1024]{1,0:T(8,128)(2,1)S(1)}, u32[]{:S(2)}, u32[]{:S(2)}) collective-permute-start(bf16[128,1024]{1,0:T(8,128)(2,1)S(1)} %get-tuple-element.93), channel_id=1, source_target_pairs={{0,6},{1,7},{2,0},{3,1},{4,2},{5,3},{6,4},{7,5},{8,14},{9,15},{10,... | collective-permute-start | bytes 786440 | tf_op jit(solution)/shard_map/ppermute | solution.py:53
  100.9 2.1 %collective-permute-start.11 = (bf16[256,1280]{1,0:T(8,128)(2,1)S(1)}, bf16[256,1280]{1,0:T(8,128)(2,1)S(1)}, u32[]{:S(2)}, u32[]{:S(2)}) collective-permute-start(bf16[256,1280]{1,0:T(8,128)(2,1)S(1)} %slice.50), channel_id=1, source_target_pairs={{0,8},{1,9},{2,10},{3,11},{4,12},{5,13},{6,14},{7,15},{8,0},{9,1},... | collective-permute-start | bytes 1966088 | tf_op jit(solution)/shard_map/ppermute | solution.py:53
  103.0 3.7 %collective-permute-done.17 = bf16[128,1024]{1,0:T(8,128)(2,1)S(1)} collective-permute-done((bf16[128,1024]{1,0:T(8,128)(2,1)S(1)}, bf16[128,1024]{1,0:T(8,128)(2,1)S(1)}, u32[]{:S(2)}, u32[]{:S(2)}) %collective-permute-start.17) | collective-permute-done | bytes 262176 | tf_op jit(solution)/shard_map/ppermute | solution.py:53
  106.8 3.4 %collective-permute-start.18 = (bf16[128,2048]{1,0:T(8,128)(2,1)S(1)}, bf16[128,2048]{1,0:T(8,128)(2,1)S(1)}, u32[]{:S(2)}, u32[]{:S(2)}) collective-permute-start(bf16[128,2048]{1,0:T(8,128)(2,1)S(1)} %pad_maximum_fusion.1), channel_id=1, source_target_pairs={{0,6},{1,7},{2,0},{3,1},{4,2},{5,3},{6,4},{7,5},{8,14},{9,15},{10,... | collective-permute-start | bytes 1572872 | tf_op jit(solution)/shard_map/ppermute | solution.py:53
  110.4 6.8 %collective-permute-done.11 = bf16[256,1280]{1,0:T(8,128)(2,1)S(1)} collective-permute-done((bf16[256,1280]{1,0:T(8,128)(2,1)S(1)}, bf16[256,1280]{1,0:T(8,128)(2,1)S(1)}, u32[]{:S(2)}, u32[]{:S(2)}) %collective-permute-start.11) | collective-permute-done | bytes 655392 | tf_op jit(solution)/shard_map/ppermute | solution.py:53
  117.6 1.3 collective-permute-start.12
  118.9 2.0 %collective-permute-start.14 = (bf16[64,2048]{1,0:T(8,128)(2,1)S(1)}, bf16[64,2048]{1,0:T(8,128)(2,1)S(1)}, u32[]{:S(2)}, u32[]{:S(2)}) collective-permute-start(bf16[64,2048]{1,0:T(8,128)(2,1)S(1)} %get-tuple-element.95), channel_id=1, source_target_pairs={{0,6},{1,7},{2,0},{3,1},{4,2},{5,3},{6,4},{7,5},{8,14},{9,15},{10,... | collective-permute-start | bytes 786440 | tf_op jit(solution)/shard_map/ppermute | solution.py:53
  122.0 4.5 %collective-permute-done.16 = bf16[128,2048]{1,0:T(8,128)(2,1)S(1)} collective-permute-done((bf16[128,2048]{1,0:T(8,128)(2,1)S(1)}, bf16[128,2048]{1,0:T(8,128)(2,1)S(1)}, u32[]{:S(2)}, u32[]{:S(2)}) %collective-permute-start.16) | collective-permute-done | bytes 524320 | tf_op jit(solution)/shard_map/ppermute | solution.py:53
  126.7 1.7 %collective-permute-start.19 = (bf16[64,2048]{1,0:T(8,128)(2,1)S(1)}, bf16[64,2048]{1,0:T(8,128)(2,1)S(1)}, u32[]{:S(2)}, u32[]{:S(2)}) collective-permute-start(bf16[64,2048]{1,0:T(8,128)(2,1)S(1)} %slice.75), channel_id=1, source_target_pairs={{0,8},{1,9},{2,10},{3,11},{4,12},{5,13},{6,14},{7,15},{8,0},{9,1},... | collective-permute-start | bytes 786440 | tf_op jit(solution)/shard_map/ppermute | solution.py:53
  128.5 6.9 %collective-permute-done.12 = bf16[64,2048]{1,0:T(8,128)(2,1)S(1)} collective-permute-done((bf16[64,2048]{1,0:T(8,128)(2,1)S(1)}, bf16[64,2048]{1,0:T(8,128)(2,1)S(1)}, u32[]{:S(2)}, u32[]{:S(2)}) %collective-permute-start.12) | collective-permute-done | bytes 262176 | tf_op jit(solution)/shard_map/ppermute | solution.py:53
  (62 shorter events, 11.9 us)
Async XLA Ops:
  0.0 9.6 %collective-permute-start.5 = (bf16[64,1024]{1,0:T(8,128)(2,1)}, bf16[64,1024]{1,0:T(8,128)(2,1)S(1)}, u32[]{:S(2)}, u32[]{:S(2)}) collective-permute-start(bf16[64,1024]{1,0:T(8,128)(2,1)} %refs_0_.1), channel_id=1, source_target_pairs={{0,10},{1,11},{2,12},{3,13},{4,14},{5,15},{6,8},{7,9},{8,2},{9,3},... | collective-permute-start | bytes 393224 | tf_op jit(solution)/shard_map/ppermute | solution.py:53
  2.9 7.8 %collective-permute-start.4 = (bf16[64,1024]{1,0:T(8,128)(2,1)}, bf16[64,1024]{1,0:T(8,128)(2,1)S(1)}, u32[]{:S(2)}, u32[]{:S(2)}) collective-permute-start(bf16[64,1024]{1,0:T(8,128)(2,1)} %refs_0_.1), channel_id=1, source_target_pairs={{0,8},{1,9},{2,10},{3,11},{4,12},{5,13},{6,14},{7,15},{8,0},{9,1},... | collective-permute-start | bytes 393224 | tf_op jit(solution)/shard_map/ppermute | solution.py:53
  3.5 14.2 %collective-permute-start.3 = (bf16[64,1024]{1,0:T(8,128)(2,1)}, bf16[64,1024]{1,0:T(8,128)(2,1)S(1)}, u32[]{:S(2)}, u32[]{:S(2)}) collective-permute-start(bf16[64,1024]{1,0:T(8,128)(2,1)} %refs_0_.1), channel_id=1, source_target_pairs={{0,4},{1,5},{2,6},{3,7},{4,0},{5,1},{6,2},{7,3},{8,12},{9,13},{10,... | collective-permute-start | bytes 393224 | tf_op jit(solution)/shard_map/ppermute | solution.py:53
  7.0 10.6 %collective-permute-start.2 = (bf16[64,1024]{1,0:T(8,128)(2,1)}, bf16[64,1024]{1,0:T(8,128)(2,1)S(1)}, u32[]{:S(2)}, u32[]{:S(2)}) collective-permute-start(bf16[64,1024]{1,0:T(8,128)(2,1)} %refs_0_.1), channel_id=1, source_target_pairs={{0,12},{1,13},{2,14},{3,15},{4,8},{5,9},{6,10},{7,11},{8,4},{9,5},... | collective-permute-start | bytes 393224 | tf_op jit(solution)/shard_map/ppermute | solution.py:53
  8.0 10.2 %collective-permute-start.1 = (bf16[64,1024]{1,0:T(8,128)(2,1)}, bf16[64,1024]{1,0:T(8,128)(2,1)S(1)}, u32[]{:S(2)}, u32[]{:S(2)}) collective-permute-start(bf16[64,1024]{1,0:T(8,128)(2,1)} %refs_0_.1), channel_id=1, source_target_pairs={{0,6},{1,7},{2,0},{3,1},{4,2},{5,3},{6,4},{7,5},{8,14},{9,15},{10,... | collective-permute-start | bytes 393224 | tf_op jit(solution)/shard_map/ppermute | solution.py:53
  9.6 8.7 %collective-permute-start = (bf16[64,1024]{1,0:T(8,128)(2,1)}, bf16[64,1024]{1,0:T(8,128)(2,1)S(1)}, u32[]{:S(2)}, u32[]{:S(2)}) collective-permute-start(bf16[64,1024]{1,0:T(8,128)(2,1)} %refs_0_.1), channel_id=1, source_target_pairs={{0,2},{1,3},{2,4},{3,5},{4,6},{5,7},{6,0},{7,1},{8,10},{9,11},{10,... | collective-permute-start | bytes 393224 | tf_op jit(solution)/shard_map/ppermute | solution.py:53
  10.7 7.6 %collective-permute-start.6 = (bf16[64,1024]{1,0:T(8,128)(2,1)}, bf16[64,1024]{1,0:T(8,128)(2,1)S(1)}, u32[]{:S(2)}, u32[]{:S(2)}) collective-permute-start(bf16[64,1024]{1,0:T(8,128)(2,1)} %refs_0_.1), channel_id=1, source_target_pairs={{0,14},{1,15},{2,8},{3,9},{4,10},{5,11},{6,12},{7,13},{8,6},{9,7},... | collective-permute-start | bytes 393224 | tf_op jit(solution)/shard_map/ppermute | solution.py:53
  14.9 4.1 %copy-start.1 = (bf16[1024,2048]{1,0:T(8,128)(2,1)S(1)}, bf16[1024,2048]{1,0:T(8,128)(2,1)}, u32[]{:S(2)}) copy-start(bf16[1024,2048]{1,0:T(8,128)(2,1)} %enc_ref.1) | copy-start | bytes 12582916
  19.0 2.7 %collective-permute-start.7 = (bf16[512,1024]{1,0:T(8,128)(2,1)S(1)}, bf16[512,1024]{1,0:T(8,128)(2,1)S(1)}, u32[]{:S(2)}, u32[]{:S(2)}) collective-permute-start(bf16[512,1024]{1,0:T(8,128)(2,1)S(1)} %shard_map.83), channel_id=1, source_target_pairs={{0,1},{1,0},{2,3},{3,2},{4,5},{5,4},{6,7},{7,6},{8,9},{9,8},{10,11... | collective-permute-start | bytes 3145736 | tf_op jit(solution)/shard_map/ppermute | solution.py:53
  21.7 51.8 %collective-permute-start.9 = (bf16[2048,4096]{1,0:T(8,128)(2,1)}, bf16[2048,4096]{1,0:T(8,128)(2,1)}, u32[]{:S(2)}, u32[]{:S(2)}) collective-permute-start(bf16[2048,4096]{1,0:T(8,128)(2,1)} %bitcast.13.w1_ref), channel_id=1, source_target_pairs={{0,1},{1,0},{2,3},{3,2},{4,5},{5,4},{6,7},{7,6},{8,9},{9,8},{10,11... | collective-permute-start | bytes 50331656 | tf_op jit(solution)/shard_map/ppermute | solution.py:53
  22.7 8.2 %copy-start.5 = (f32[2048]{0:T(1024)S(1)}, f32[2048]{0:T(1024)}, u32[]{:S(2)}) copy-start(f32[2048]{0:T(1024)} %param.15) | copy-start | bytes 24580
  66.9 3.5 %collective-permute-start.8 = (bf16[6144,128]{1,0:T(8,128)(2,1)S(1)}, bf16[6144,128]{1,0:T(8,128)(2,1)S(1)}, u32[]{:S(2)}, u32[]{:S(2)}) collective-permute-start(bf16[6144,128]{1,0:T(8,128)(2,1)S(1)} %get-tuple-element.97.act_ref), channel_id=1, source_target_pairs={{0,1},{1,0},{2,3},{3,2},{4,5},{5,4},{6,7},{7,6},{8,9},{9,8},{10,11... | collective-permute-start | bytes 4718600 | tf_op jit(solution)/shard_map/ppermute | solution.py:53
  85.3 12.6 %collective-permute-start.10 = (bf16[256,768]{1,0:T(8,128)(2,1)S(1)}, bf16[256,768]{1,0:T(8,128)(2,1)S(1)}, u32[]{:S(2)}, u32[]{:S(2)}) collective-permute-start(bf16[256,768]{1,0:T(8,128)(2,1)S(1)} %slice.51), channel_id=1, source_target_pairs={{0,8},{1,9},{2,10},{3,11},{4,12},{5,13},{6,14},{7,15},{8,0},{9,1},... | collective-permute-start | bytes 1179656 | tf_op jit(solution)/shard_map/ppermute | solution.py:53
  85.9 14.9 %copy-start.6 = (s32[64]{0:T(128)S(1)}, s32[64]{0:T(128)}, u32[]{:S(2)}) copy-start(s32[64]{0:T(128)} %param.19) | copy-start | bytes 772
  97.9 8.8 %collective-permute-start.17 = (bf16[128,1024]{1,0:T(8,128)(2,1)S(1)}, bf16[128,1024]{1,0:T(8,128)(2,1)S(1)}, u32[]{:S(2)}, u32[]{:S(2)}) collective-permute-start(bf16[128,1024]{1,0:T(8,128)(2,1)S(1)} %get-tuple-element.93), channel_id=1, source_target_pairs={{0,6},{1,7},{2,0},{3,1},{4,2},{5,3},{6,4},{7,5},{8,14},{9,15},{10,... | collective-permute-start | bytes 786440 | tf_op jit(solution)/shard_map/ppermute | solution.py:53
  100.8 9.4 %collective-permute-start.15 = (bf16[128,1024]{1,0:T(8,128)(2,1)S(1)}, bf16[128,1024]{1,0:T(8,128)(2,1)S(1)}, u32[]{:S(2)}, u32[]{:S(2)}) collective-permute-start(bf16[128,1024]{1,0:T(8,128)(2,1)S(1)} %get-tuple-element.91), channel_id=1, source_target_pairs={{0,2},{1,3},{2,4},{3,5},{4,6},{5,7},{6,0},{7,1},{8,10},{9,11},{10,... | collective-permute-start | bytes 786440 | tf_op jit(solution)/shard_map/ppermute | solution.py:53
  100.9 16.3 %collective-permute-start.11 = (bf16[256,1280]{1,0:T(8,128)(2,1)S(1)}, bf16[256,1280]{1,0:T(8,128)(2,1)S(1)}, u32[]{:S(2)}, u32[]{:S(2)}) collective-permute-start(bf16[256,1280]{1,0:T(8,128)(2,1)S(1)} %slice.50), channel_id=1, source_target_pairs={{0,8},{1,9},{2,10},{3,11},{4,12},{5,13},{6,14},{7,15},{8,0},{9,1},... | collective-permute-start | bytes 1966088 | tf_op jit(solution)/shard_map/ppermute | solution.py:53
  106.8 15.2 %collective-permute-start.18 = (bf16[128,2048]{1,0:T(8,128)(2,1)S(1)}, bf16[128,2048]{1,0:T(8,128)(2,1)S(1)}, u32[]{:S(2)}, u32[]{:S(2)}) collective-permute-start(bf16[128,2048]{1,0:T(8,128)(2,1)S(1)} %pad_maximum_fusion.1), channel_id=1, source_target_pairs={{0,6},{1,7},{2,0},{3,1},{4,2},{5,3},{6,4},{7,5},{8,14},{9,15},{10,... | collective-permute-start | bytes 1572872 | tf_op jit(solution)/shard_map/ppermute | solution.py:53
  110.3 16.1 %collective-permute-start.16 = (bf16[128,2048]{1,0:T(8,128)(2,1)S(1)}, bf16[128,2048]{1,0:T(8,128)(2,1)S(1)}, u32[]{:S(2)}, u32[]{:S(2)}) collective-permute-start(bf16[128,2048]{1,0:T(8,128)(2,1)S(1)} %pad_maximum_fusion), channel_id=1, source_target_pairs={{0,2},{1,3},{2,4},{3,5},{4,6},{5,7},{6,0},{7,1},{8,10},{9,11},{10,... | collective-permute-start | bytes 1572872 | tf_op jit(solution)/shard_map/ppermute | solution.py:53
  117.6 17.8 %collective-permute-start.12 = (bf16[64,2048]{1,0:T(8,128)(2,1)S(1)}, bf16[64,2048]{1,0:T(8,128)(2,1)S(1)}, u32[]{:S(2)}, u32[]{:S(2)}) collective-permute-start(bf16[64,2048]{1,0:T(8,128)(2,1)S(1)} %get-tuple-element.94), channel_id=1, source_target_pairs={{0,2},{1,3},{2,4},{3,5},{4,6},{5,7},{6,0},{7,1},{8,10},{9,11},{10,... | collective-permute-start | bytes 786440 | tf_op jit(solution)/shard_map/ppermute | solution.py:53
  118.9 16.5 %collective-permute-start.14 = (bf16[64,2048]{1,0:T(8,128)(2,1)S(1)}, bf16[64,2048]{1,0:T(8,128)(2,1)S(1)}, u32[]{:S(2)}, u32[]{:S(2)}) collective-permute-start(bf16[64,2048]{1,0:T(8,128)(2,1)S(1)} %get-tuple-element.95), channel_id=1, source_target_pairs={{0,6},{1,7},{2,0},{3,1},{4,2},{5,3},{6,4},{7,5},{8,14},{9,15},{10,... | collective-permute-start | bytes 786440 | tf_op jit(solution)/shard_map/ppermute | solution.py:53
  120.9 14.5 %collective-permute-start.13 = (bf16[64,2048]{1,0:T(8,128)(2,1)S(1)}, bf16[64,2048]{1,0:T(8,128)(2,1)S(1)}, u32[]{:S(2)}, u32[]{:S(2)}) collective-permute-start(bf16[64,2048]{1,0:T(8,128)(2,1)S(1)} %get-tuple-element.96), channel_id=1, source_target_pairs={{0,4},{1,5},{2,6},{3,7},{4,0},{5,1},{6,2},{7,3},{8,12},{9,13},{10,... | collective-permute-start | bytes 786440 | tf_op jit(solution)/shard_map/ppermute | solution.py:53
  126.7 8.9 %copy-start.4 = (bf16[1,64,4096]{2,1,0:T(8,128)(2,1)S(1)}, bf16[1,64,4096]{2,1,0:T(8,128)(2,1)}, u32[]{:S(2)}) copy-start(bf16[1,64,4096]{2,1,0:T(8,128)(2,1)} %param.17) | copy-start | bytes 1572868
  126.7 8.8 %collective-permute-start.19 = (bf16[64,2048]{1,0:T(8,128)(2,1)S(1)}, bf16[64,2048]{1,0:T(8,128)(2,1)S(1)}, u32[]{:S(2)}, u32[]{:S(2)}) collective-permute-start(bf16[64,2048]{1,0:T(8,128)(2,1)S(1)} %slice.75), channel_id=1, source_target_pairs={{0,8},{1,9},{2,10},{3,11},{4,12},{5,13},{6,14},{7,15},{8,0},{9,1},... | collective-permute-start | bytes 786440 | tf_op jit(solution)/shard_map/ppermute | solution.py:53
  (3 other events, 5.0 us)
